TPU v7x, 32 devices: a whole 2x2x4 slice. The times are simulated.
32 devices in a mesh: seq: 8 (over y, x, core), exp: 4 (over z).
Axes of the slice: x: 2, y: 2, z: 4, core: 2. Of those that a mesh axis runs over, the one named last changes fastest.
Arguments:
- tokens: bfloat16 [1024, 2304], P('seq'), may hold values from -6 to 6
- norm_gain: bfloat16 [2304], replicated, may hold values from 0.099609375 to 1.8984375
- w_qkv: bfloat16 [2304, 3, 2048], P(None, None, 'exp'), may hold values from -12 to 12
- w_out: bfloat16 [2048, 2304], P('exp'), may hold values from -0.125 to 0.125
- moe_gain: bfloat16 [2304], replicated, may hold values from 0.099609375 to 1.8984375
- w_router: bfloat16 [2304, 4], replicated, may hold values from -0.25 to 0.25
- gate_up: bfloat16 [4, 2, 2304, 5760], P('exp', None, None, 'seq'), may hold values from -0.125 to 0.125
- w_down: bfloat16 [4, 5760, 2304], P('exp', 'seq'), may hold values from -0.078125 to 0.078125
- lengths: int32 [4], replicated, may hold values from 1 to 768, as said below
- blocks_seen: int32 [8, 8], P('seq'), may hold values from 0 to 1, as said below
- expert_ids: int32 [1024, 2], P(('seq', 'exp')), may hold values from 0 to 3, all different within a row; in each aligned block of 32 rows (0 to 31, 32 to 63, ...) at most 32 rows name the same one
- old_place: int32 [4], replicated, may hold values from 0 to 3, each once
- new_place: int32 [4], replicated, may hold values from 0 to 3, each once
Outputs:
- layer_out: bfloat16 [1024, 2304], P(('seq', 'exp'))
- new_gate_up: bfloat16 [4, 2, 2304, 5760], P('exp', None, None, 'seq')
- new_down: bfloat16 [4, 5760, 2304], P('exp', 'seq')
Inputs may be any that keep to these rules, and one draw needn't show every extreme that they name: `lengths`: positive, summing to 1024, the largest exactly 768. `blocks_seen`: 1 on the diagonal; 0 above it and wherever no sequence has tokens in both blocks; elsewhere 0 or 1. `expert_ids`: the two experts of a token differ; among the 32 tokens of one device no expert is named more than 32 times, and in some devices one expert exactly 32 times. `old_place`: a permutation of the experts. `new_place`: a permutation of the experts.
All inputs are finite; a program needn't handle non-finite values.
Results may differ from a plain program's by a relative error of at most 0.023.
Values may be sent and summed in bfloat16 or wider, within the bound.
A program may use at most 128 MiB of HBM per device.

v0:
```python
import jax
import jax.numpy as jnp
from jax import lax
from jax.sharding import PartitionSpec as P

HEAD_DIM = 64


epsilon = 1e-05
masked_score = -1e30


def rms_scale(values_in, gain):
    widened = values_in.astype(jnp.float32)
    inverse = lax.rsqrt(jnp.mean(widened * widened, axis=-1, keepdims=True) + epsilon)
    return widened * inverse * gain.astype(jnp.float32)


def rotate(vectors, angle_base):
    halfway = vectors.shape[-1] // 2
    spacing = jnp.arange(halfway, dtype=jnp.float32) / halfway
    freqs_all = jnp.exp(-jnp.log(10000.0) * spacing)
    angles = angle_base[:, None] * freqs_all[None, :]
    cosine = jnp.cos(angles)[:, None, :]
    sine_part = jnp.sin(angles)[:, None, :]
    leading = vectors[..., :halfway]
    trailing = vectors[..., halfway:]
    return jnp.concatenate(
        [leading * cosine - trailing * sine_part, trailing * cosine + leading * sine_part], axis=-1
    )


def doc_layout(seq_lengths, row_ids):
    ending = jnp.cumsum(seq_lengths, dtype=jnp.int32)
    passed = (ending[None, :] <= row_ids[:, None]).astype(jnp.int32)
    doc_ids = jnp.sum(passed, axis=1, dtype=jnp.int32)
    starting = jnp.sum(passed * seq_lengths[None, :], axis=1, dtype=jnp.int32)
    return (doc_ids, row_ids - starting)


def owner_table(placing):
    slot_range = jnp.arange(placing.shape[0], dtype=jnp.int32)
    return jnp.sum(
        jnp.where(placing[:, None] == slot_range[None, :], slot_range[:, None], 0),
        axis=0,
        dtype=jnp.int32,
    )


def attend_block(
    carried,
    queries,
    query_rows,
    query_docs,
    key_block,
    value_block,
    key_rows,
    seq_lengths,
    seen_row,
    block_rows,
):
    key_docs, _ = doc_layout(seq_lengths, key_rows)
    key_blocks = jnp.floor_divide(key_rows, block_rows)
    block_range = jnp.arange(seen_row.shape[0], dtype=jnp.int32)
    key_seen = (
        jnp.sum(
            jnp.where(key_blocks[:, None] == block_range[None, :], seen_row[None, :], 0),
            axis=1,
            dtype=jnp.int32,
        )
        > 0
    )
    allowed = (
        (query_docs[:, None] == key_docs[None, :])
        & (key_rows[None, :] <= query_rows[:, None])
        & key_seen[None, :]
    )
    score_scale = queries.shape[-1] ** (-0.5)

    def compute(state_in):
        largest, totals, summed = state_in
        scores = (
            jnp.einsum("qhd,khd->hqk", queries, key_block, preferred_element_type=jnp.float32)
            * score_scale
        )
        scores = jnp.where(allowed[None], scores, masked_score)
        new_largest = jnp.maximum(largest, jnp.max(scores, axis=2))
        weights = jnp.where(allowed[None], jnp.exp(scores - new_largest[:, :, None]), 0.0)
        totals = jnp.sum(weights, axis=2)
        summed = jnp.einsum(
            "hqk,khd->hqd",
            weights.astype(jnp.bfloat16),
            value_block,
            preferred_element_type=jnp.float32,
        )
        return (new_largest, totals, summed)

    def unchanged(state_in):
        return state_in

    return lax.cond(jnp.any(allowed), compute, unchanged, carried)


def shards(
    tokens,
    norm_gain,
    w_qkv,
    w_out,
    moe_gain,
    w_router,
    gate_up,
    w_down,
    lengths,
    blocks_seen,
    expert_ids,
    old_place,
    new_place,
):
    block_rows = tokens.shape[0]
    model_width = tokens.shape[1]
    exp_count = lax.axis_size("exp")
    block_index = lax.axis_index("seq")
    slot_index = lax.axis_index("exp")
    heads_here = w_qkv.shape[2] // HEAD_DIM
    query_rows = block_index * block_rows + jnp.arange(block_rows, dtype=jnp.int32)
    query_docs, query_places = doc_layout(lengths, query_rows)
    normed = rms_scale(tokens, norm_gain).astype(jnp.bfloat16)
    projected = jnp.dot(
        normed,
        w_qkv.reshape(model_width, 3 * heads_here * HEAD_DIM),
        preferred_element_type=jnp.float32,
    )
    projected = projected.reshape(block_rows, 3, heads_here, HEAD_DIM)
    angle_rows = query_places.astype(jnp.float32)
    queries = rotate(projected[:, 0], angle_rows).astype(jnp.bfloat16)
    key_block = rotate(projected[:, 1], angle_rows).astype(jnp.bfloat16)
    value_block = projected[:, 2].astype(jnp.bfloat16)
    seen_row = blocks_seen[0]
    initial = (
        jnp.full((heads_here, block_rows), masked_score, jnp.float32),
        jnp.zeros((heads_here, block_rows), jnp.float32),
        jnp.zeros((heads_here, block_rows, HEAD_DIM), jnp.float32),
    )
    pieces = (
        lax.all_gather(key_block, "seq", axis=0, tiled=True),
        lax.all_gather(value_block, "seq", axis=0, tiled=True),
    )
    key_rows = jnp.arange(pieces[0].shape[0], dtype=jnp.int32)
    largest, totals, summed = attend_block(
        initial,
        queries,
        query_rows,
        query_docs,
        pieces[0],
        pieces[1],
        key_rows,
        lengths,
        seen_row,
        block_rows,
    )
    attended = (summed / totals[:, :, None]).astype(jnp.bfloat16)
    attended = jnp.transpose(attended, (1, 0, 2)).reshape(block_rows, heads_here * HEAD_DIM)
    shard_rows = block_rows // exp_count
    rows_in = attended
    head_total = lax.psum_scatter(
        jnp.dot(rows_in, w_out, preferred_element_type=jnp.float32).astype(jnp.bfloat16),
        "exp",
        scatter_dimension=0,
        tiled=True,
    ).astype(jnp.float32)
    residual = lax.dynamic_slice_in_dim(tokens, slot_index * shard_rows, shard_rows, 0)
    hidden = (residual.astype(jnp.float32) + head_total).astype(jnp.bfloat16)
    moe_in = rms_scale(hidden, moe_gain).astype(jnp.bfloat16)
    logits = jnp.dot(moe_in, w_router, preferred_element_type=jnp.float32)
    expert_count = w_router.shape[1]
    expert_range = jnp.arange(expert_count, dtype=jnp.int32)
    chosen = jnp.sum(
        jnp.where(expert_ids[:, :, None] == expert_range[None, None, :], logits[:, None, :], 0.0),
        axis=2,
    )
    gate_first = 1.0 / (1.0 + jnp.exp(chosen[:, 1] - chosen[:, 0]))
    gate_second = 1.0 / (1.0 + jnp.exp(chosen[:, 0] - chosen[:, 1]))
    gating = jnp.stack([gate_first, gate_second], axis=1)
    slot_old = owner_table(old_place)
    source_slot = jnp.sum(
        jnp.where(new_place[:, None] == expert_range[None, :], slot_old[None, :], 0),
        axis=1,
        dtype=jnp.int32,
    )
    slice_width = gate_up.shape[3]
    piece_width = model_width // exp_count
    gate_split = gate_up.reshape(2, exp_count, piece_width, slice_width)
    down_split = w_down.reshape(slice_width, exp_count, piece_width)
    gate_held, down_held = (
        lax.all_to_all(gate_split, "exp", split_axis=1, concat_axis=1, tiled=True),
        lax.all_to_all(down_split, "exp", split_axis=1, concat_axis=1, tiled=True),
    )
    gate_sorted = jnp.take(gate_held, source_slot, axis=1)
    down_sorted = jnp.take(down_held, source_slot, axis=1)
    gate_moved, down_moved = (
        lax.all_to_all(gate_sorted, "exp", split_axis=1, concat_axis=1, tiled=True),
        lax.all_to_all(down_sorted, "exp", split_axis=1, concat_axis=1, tiled=True),
    )
    new_gate_up = gate_moved.reshape(1, 2, model_width, slice_width)
    new_down = down_moved.reshape(1, slice_width, model_width)
    owners = owner_table(new_place)
    column_gate = new_gate_up[0]
    column_down = new_down[0]
    capacity = min(shard_rows, 4 * shard_rows // exp_count)
    slot_total = exp_count * capacity
    pair_ids = expert_ids.reshape(-1)
    pair_marks = (pair_ids[:, None] == expert_range[None, :]).astype(jnp.int32)
    earlier = jnp.cumsum(pair_marks, axis=0, dtype=jnp.int32) - pair_marks
    rank_in = jnp.sum(earlier * pair_marks, axis=1, dtype=jnp.int32)
    owner_of = jnp.sum(pair_marks * owners[None, :], axis=1, dtype=jnp.int32)
    target = owner_of * capacity + rank_in
    selector = target[:, None] == jnp.arange(slot_total, dtype=jnp.int32)[None, :]
    repeated = jnp.repeat(moe_in, 2, axis=0)
    outgoing = jnp.einsum(
        "as,ad->sd", selector.astype(jnp.bfloat16), repeated, preferred_element_type=jnp.float32
    )
    outgoing = outgoing.astype(jnp.bfloat16).reshape(exp_count, capacity, model_width)
    arrived = lax.all_to_all(outgoing, "exp", split_axis=0, concat_axis=0, tiled=True)
    source_count = arrived.shape[0]
    item_count = arrived.shape[1]
    pieces = lax.all_gather(arrived, "seq", axis=0, tiled=True)
    flat_rows = pieces.reshape(-1, model_width)
    projected_pair = jnp.einsum(
        "rd,cdf->crf", flat_rows, column_gate, preferred_element_type=jnp.float32
    )
    activated = (jax.nn.silu(projected_pair[0]) * projected_pair[1]).astype(jnp.bfloat16)
    hidden_all = activated.reshape(pieces.shape[0], item_count, slice_width)
    rows_in = hidden_all
    flat_out = jnp.dot(
        rows_in.reshape(-1, slice_width), column_down, preferred_element_type=jnp.float32
    )
    column_sum = lax.psum_scatter(
        flat_out.reshape(source_count * lax.axis_size("seq"), item_count, model_width).astype(
            jnp.bfloat16
        ),
        "seq",
        scatter_dimension=0,
        tiled=True,
    )
    returned = lax.all_to_all(column_sum, "exp", split_axis=0, concat_axis=0, tiled=True)
    pair_gates = gating.reshape(-1)
    spread = jnp.sum(
        jnp.where(selector, pair_gates[:, None], 0.0).reshape(shard_rows, 2, slot_total), axis=1
    )
    moe_sum = jnp.dot(
        spread,
        returned.reshape(slot_total, model_width).astype(jnp.float32),
        precision=lax.Precision.HIGHEST,
    )
    layer_out = (hidden.astype(jnp.float32) + moe_sum).astype(jnp.bfloat16)
    return (layer_out, new_gate_up, new_down)


def solution(mesh):
    in_specs = (
        P("seq", None),
        P(),
        P(None, None, "exp"),
        P("exp", None),
        P(),
        P(),
        P("exp", None, None, "seq"),
        P("exp", "seq", None),
        P(),
        P("seq", None),
        P(("seq", "exp"), None),
        P(),
        P(),
    )
    out_specs = (P(("seq", "exp"), None), P("exp", None, None, "seq"), P("exp", "seq", None))
    return jax.shard_map(shards, mesh=mesh, in_specs=in_specs, out_specs=out_specs, check_vma=False)
```

profile of v0, /device:TPU:0, one launch (start us, length us, event | category | flops | bytes accessed | tf_op | source)
XLA Modules:
  0.0 705.8 jit_solution(3215357129736925727)
XLA Ops:
  7.3 9.9 %copy.49 = bf16[2304,3,512]{0,2,1:T(8,128)(2,1)} copy(bf16[2304,3,512]{2,0,1:T(8,128)(2,1)} %param.17) | data formatting | bytes 14155776 | tf_op args[2]
  17.4 5.3 fusion.15
  28.1 23.9 %all-gather.5.cloned.1.call-done = bf16[1024,8,64]{0,2,1:T(8,128)(2,1)} async-done(((bf16[128,8,64]{0,2,1:T(8,128)(2,1)}), bf16[1024,8,64]{0,2,1:T(8,128)(2,1)}) %all-gather.5.cloned.1.call-update) | async-done | bytes 1048592 | tf_op jit(solution)/shard_map/all_gather | solution.py:145
  52.0 26.1 %all-gather.9.cloned.1.call-done = bf16[1024,1,8,64]{0,3,2,1:T(8,128)(2,1)} async-done(((bf16[128,1,8,64]{0,3,2,1:T(8,128)(2,1)}), bf16[1024,1,8,64]{0,3,2,1:T(8,128)(2,1)}) %all-gather.9.cloned.1.call-update) | async-done | bytes 1048592 | tf_op jit(solution)/shard_map/all_gather | solution.py:146
  78.1 4.9 conditional.1
  78.1 2.3 fusion
  83.1 1.3 convolution_convert_fusion.2
  85.3 21.3 %reduce-scatter.3.cloned.1.call-done = bf16[32,2304]{1,0:T(8,128)(2,1)} async-done(((bf16[128,2304]{1,0:T(8,128)(2,1)}), bf16[32,2304]{1,0:T(8,128)(2,1)}) %reduce-scatter.3.cloned.1.call-update) | async-done | bytes 147472 | tf_op jit(solution)/shard_map/reduce_scatter | solution.py:165
  109.4 3.5 all-to-all-start.2
  112.9 10.2 %copy.52 = bf16[1,2,2304,720]{3,2,1,0:T(8,128)(2,1)} copy(bf16[1,2,2304,720]{2,3,1,0:T(8,128)(2,1)} %param.21) | data formatting | bytes 13271040 | tf_op args[6]
  123.1 6.4 copy.53
  130.3 5.4 all-to-all-start
  135.7 5.7 copy.57
  141.4 147.5 %all-to-all-done = bf16[2,4,576,720]{3,2,0,1:T(8,128)(2,1)} async-done(((bf16[2,4,576,720]{3,2,0,1:T(8,128)(2,1)}), bf16[2,4,576,720]{3,2,0,1:T(8,128)(2,1)}, u32[]{:S(2)}, u32[]{:S(2)}) %all-to-all-start) | async-done | bytes 6635552 | tf_op jit(solution)/shard_map/all_to_all | solution.py:195
  288.9 4.7 all-to-all-start.3
  293.7 6.9 gather_fusion
  300.6 6.7 select_bitcast_fusion
  307.3 65.0 %all-to-all-done.3 = bf16[720,4,576]{0,2,1:T(8,128)(2,1)} async-done(((bf16[720,4,576]{0,2,1:T(8,128)(2,1)}), bf16[720,4,576]{0,2,1:T(8,128)(2,1)}, u32[]{:S(2)}, u32[]{:S(2)}) %all-to-all-start.3) | async-done | bytes 3317792 | tf_op jit(solution)/shard_map/all_to_all | solution.py:196
  372.3 5.4 all-to-all-start.1
  378.3 4.6 gather_fusion.1
  382.8 4.2 select_bitcast_fusion.1
  387.0 145.1 %all-to-all-done.1 = bf16[2,4,576,720]{3,2,0,1:T(8,128)(2,1)} async-done(((bf16[2,4,576,720]{3,2,0,1:T(8,128)(2,1)}), bf16[2,4,576,720]{3,2,0,1:T(8,128)(2,1)}, u32[]{:S(2)}, u32[]{:S(2)}) %all-to-all-start.1) | async-done | bytes 6635552 | tf_op jit(solution)/shard_map/all_to_all | solution.py:201
  532.2 4.7 all-to-all-start.4
  537.1 6.4 copy.54
  543.5 11.5 %convolution_bitcast_fusion = f32[2,1024,720]{1,2,0:T(8,128)S(1)} fusion(bf16[2,2304,720]{2,1,0:T(8,128)(2,1)} %bitcast.61, bf16[1024,2304,1]{1,0,2:T(8,128)(2,1)} %bitcast.72), kind=kOutput, calls=%fused_computation.22 | convolution fusion | flops 6794772480 | bytes 17252352 | tf_op jit(solution)/shard_map/rd,cdf->crf/dot_general | solution.py:228
  556.0 1.6 copy.56
  557.6 58.0 %all-to-all-done.4 = bf16[720,4,576]{0,2,1:T(8,128)(2,1)} async-done(((bf16[720,4,576]{0,2,1:T(8,128)(2,1)}), bf16[720,4,576]{0,2,1:T(8,128)(2,1)}, u32[]{:S(2)}, u32[]{:S(2)}) %all-to-all-start.4) | async-done | bytes 3317792 | tf_op jit(solution)/shard_map/all_to_all | solution.py:202
  615.6 8.5 %convolution_convert_fusion = bf16[32,32,2304]{2,1,0:T(8,128)(2,1)} fusion(bf16[32,32,720]{2,1,0:T(8,128)(2,1)} %bitcast.66, bf16[720,2304,1]{0,1,2:T(8,128)(2,1)} %bitcast.26), kind=kOutput, calls=%fused_computation.14 | convolution fusion | flops 3399745536 | bytes 9510912 | tf_op jit(solution)/shard_map/dot_general | solution.py:234
  624.1 53.1 %reduce-scatter.5.cloned.1.call-done = bf16[4,32,2304]{2,1,0:T(8,128)(2,1)} async-done(((bf16[32,32,2304]{2,1,0:T(8,128)(2,1)}), bf16[4,32,2304]{2,1,0:T(8,128)(2,1)}) %reduce-scatter.5.cloned.1.call-update) | async-done | bytes 589840 | tf_op jit(solution)/shard_map/reduce_scatter | solution.py:237
  677.2 4.6 all-to-all-start.5
  682.3 5.6 copy.61
  687.9 10.3 %copy.60 = bf16[1,2,2304,720]{2,3,1,0:T(8,128)(2,1)} copy(bf16[1,2,2304,720]{3,2,1,0:T(8,128)(2,1)} %bitcast.62) | data formatting | bytes 13271040
  (89 shorter events, 15.4 us)
Async XLA Ops:
  7.2 75.9 %copy-start = (bf16[512,2304]{1,0:T(8,128)(2,1)S(1)}, bf16[512,2304]{1,0:T(8,128)(2,1)}, u32[]{:S(2)}) copy-start(bf16[512,2304]{1,0:T(8,128)(2,1)} %param.18) | copy-start | bytes 7077892
  7.2 44.9 %all-gather.5.cloned.1.call-start = ((), (), s32[]{:S(2)}) async-start(), calls=%async_computation.8 | async-start | bytes 1179648 | tf_op jit(solution)/shard_map/all_gather | solution.py:145
  7.3 9.9 %copy-start.4 = (bf16[2304]{0:T(1024)(128)(2,1)S(1)}, bf16[2304]{0:T(1024)(128)(2,1)}, u32[]{:S(2)}) copy-start(bf16[2304]{0:T(1024)(128)(2,1)} %param.16) | copy-start | bytes 13828
  7.3 9.9 %copy-start.2 = (bf16[128,2304]{1,0:T(8,128)(2,1)S(1)}, bf16[128,2304]{1,0:T(8,128)(2,1)}, u32[]{:S(2)}) copy-start(bf16[128,2304]{1,0:T(8,128)(2,1)} %param.15) | copy-start | bytes 1769476
  17.4 6.1 copy-start.7
  17.4 9.1 %copy-start.8 = (s32[1,8]{1,0:T(1,128)S(1)}, s32[1,8]{1,0:T(1,128)}, u32[]{:S(2)}) copy-start(s32[1,8]{1,0:T(1,128)} %param.24) | copy-start | bytes 100
  25.6 52.5 %all-gather.9.cloned.1.call-start = ((), (), s32[]{:S(2)}) async-start(), calls=%async_computation.12 | async-start | bytes 1179648 | tf_op jit(solution)/shard_map/all_gather | solution.py:146
  26.4 80.2 %reduce-scatter.3.cloned.1.call-start = ((), (), s32[]{:S(2)}) async-start(), calls=%async_computation.9 | async-start | bytes 737280 | tf_op jit(solution)/shard_map/reduce_scatter | solution.py:165
  78.1 6.4 copy-start.5
  78.1 6.4 copy-start.6
  78.1 3.6 copy-start.10
  83.0 1.8 copy-start.12
  83.0 1.9 copy-start.9
  109.4 20.1 %all-to-all-start.2 = ((bf16[4,32,2304]{2,1,0:T(8,128)(2,1)}), bf16[4,32,2304]{2,1,0:T(8,128)(2,1)S(1)}, u32[]{:S(2)}, u32[]{:S(2)}) async-start(bf16[4,32,2304]{2,1,0:T(8,128)(2,1)} %bitcast.18), calls=%async_computation.3 | async-start | bytes 1179648 | tf_op jit(solution)/shard_map/all_to_all | solution.py:223
  129.5 0.8 copy-start.3
  130.3 158.6 %all-to-all-start = ((bf16[2,4,576,720]{3,2,0,1:T(8,128)(2,1)}), bf16[2,4,576,720]{3,2,0,1:T(8,128)(2,1)}, u32[]{:S(2)}, u32[]{:S(2)}) async-start(bf16[2,4,576,720]{3,2,0,1:T(8,128)(2,1)} %copy.53), calls=%async_computation.1 | async-start | bytes 14155776 | tf_op jit(solution)/shard_map/all_to_all | solution.py:195
  288.9 83.4 %all-to-all-start.3 = ((bf16[720,4,576]{0,2,1:T(8,128)(2,1)}), bf16[720,4,576]{0,2,1:T(8,128)(2,1)}, u32[]{:S(2)}, u32[]{:S(2)}) async-start(bf16[720,4,576]{0,2,1:T(8,128)(2,1)} %bitcast.64), calls=%async_computation.4 | async-start | bytes 7077888 | tf_op jit(solution)/shard_map/all_to_all | solution.py:196
  372.3 159.9 %all-to-all-start.1 = ((bf16[2,4,576,720]{3,2,0,1:T(8,128)(2,1)}), bf16[2,4,576,720]{3,2,0,1:T(8,128)(2,1)}, u32[]{:S(2)}, u32[]{:S(2)}) async-start(bf16[2,4,576,720]{3,2,0,1:T(8,128)(2,1)} %select_bitcast_fusion), calls=%async_computation.2 | async-start | bytes 14155776 | tf_op jit(solution)/shard_map/all_to_all | solution.py:201
  377.7 165.9 %all-gather.7.cloned.1.call-start = ((), (), s32[]{:S(2)}) async-start(), calls=%async_computation.10 | async-start | bytes 5308416 | tf_op jit(solution)/shard_map/all_gather | solution.py:226
  532.2 83.4 %all-to-all-start.4 = ((bf16[720,4,576]{0,2,1:T(8,128)(2,1)}), bf16[720,4,576]{0,2,1:T(8,128)(2,1)}, u32[]{:S(2)}, u32[]{:S(2)}) async-start(bf16[720,4,576]{0,2,1:T(8,128)(2,1)} %select_bitcast_fusion.1), calls=%async_computation.5 | async-start | bytes 7077888 | tf_op jit(solution)/shard_map/all_to_all | solution.py:202
  536.9 140.3 %reduce-scatter.5.cloned.1.call-start = ((), (), s32[]{:S(2)}) async-start(), calls=%async_computation.11 | async-start | bytes 5308416 | tf_op jit(solution)/shard_map/reduce_scatter | solution.py:237
  624.1 57.9 %copy-start.11 = (bf16[2304,4]{0,1:T(4,128)(2,1)S(1)}, bf16[2304,4]{0,1:T(4,128)(2,1)}, u32[]{:S(2)}) copy-start(bf16[2304,4]{0,1:T(4,128)(2,1)} %param.20) | copy-start | bytes 55300
  677.2 21.0 %all-to-all-start.5 = ((bf16[4,32,2304]{2,1,0:T(8,128)(2,1)}), bf16[4,32,2304]{2,1,0:T(8,128)(2,1)S(1)}, u32[]{:S(2)}, u32[]{:S(2)}) async-start(bf16[4,32,2304]{2,1,0:T(8,128)(2,1)} %reduce-scatter.5.cloned.1.call-done), calls=%async_computation.7 | async-start | bytes 1179648 | tf_op jit(solution)/shard_map/all_to_all | solution.py:245
  687.9 11.3 %copy-start.1 = (bf16[512,2304]{1,0:T(8,128)(2,1)S(1)}, bf16[512,2304]{1,0:T(8,128)(2,1)}, u32[]{:S(2)}) copy-start(bf16[512,2304]{1,0:T(8,128)(2,1)} %param.18) | copy-start | bytes 7077892
Sparse Core Ops, SparseCore 0:
  25.7 26.2 all-gather.4
  54.5 23.5 all-gather.8
  84.6 21.9 reduce-scatter.2
  380.7 40.2 all-gather.6
  624.2 52.9 reduce-scatter.4
where the time goes:
time: 707 us; the launch traced here: 706 us
  waiting for transfers between devices  541 us (77%)
  local copies, waits for them, and re-layouts  70.5 us (10%)
  matrix products  32.7 us (5%)
  starting transfers between devices  28.7 us (4%)
  other arithmetic  18.6 us (3%)
  between operations  14.8 us (2%)
    all_to_all x1, waiting for transfers between devices, shards(): lax.all_to_all(gate_split, 'exp', split_axis=1, concat_axis=1, tiled=True)  148 us
    all_to_all x1, waiting for transfers between devices, shards(): lax.all_to_all(gate_sorted, 'exp', split_axis=1, concat_axis=1, tiled=True)  145 us
    all_to_all x1, waiting for transfers between devices, shards(): lax.all_to_all(down_split, 'exp', split_axis=1, concat_axis=1, tiled=True)  65 us
    all_to_all x1, waiting for transfers between devices, shards(): lax.all_to_all(down_sorted, 'exp', split_axis=1, concat_axis=1, tiled=True)  58 us
    reduce_scatter x1, waiting for transfers between devices, shards(): lax.psum_scatter(flat_out.reshape(source_count * lax.axis_size('seq'), it...  53.1 us
    unnamed x30, local copies, waits for them, and re-layouts  42.6 us
    all_gather x1, waiting for transfers between devices, shards(): lax.all_gather(value_block, 'seq', axis=0, tiled=True)  26.1 us
    all_gather x1, waiting for transfers between devices, shards(): lax.all_gather(key_block, 'seq', axis=0, tiled=True)  23.9 us
  transfers between devices with their start and end apart: 11, of which 8 were waited for; matrix products, arithmetic and copies ran while one was open for 12% of the time, Pallas kernels for 0%

commit v1 on v0

v1 whole, which is shorter than its diff:
```python
import jax
import jax.numpy as jnp
from jax import lax
from jax.sharding import PartitionSpec as P

HEAD_DIM = 64


epsilon = 1e-05
masked_score = -1e30


def rms_scale(values_in, gain):
    widened = values_in.astype(jnp.float32)
    inverse = lax.rsqrt(jnp.mean(widened * widened, axis=-1, keepdims=True) + epsilon)
    return widened * inverse * gain.astype(jnp.float32)


def rotate(vectors, angle_base):
    halfway = vectors.shape[-1] // 2
    spacing = jnp.arange(halfway, dtype=jnp.float32) / halfway
    freqs_all = jnp.exp(-jnp.log(10000.0) * spacing)
    angles = angle_base[:, None] * freqs_all[None, :]
    cosine = jnp.cos(angles)[:, None, :]
    sine_part = jnp.sin(angles)[:, None, :]
    leading = vectors[..., :halfway]
    trailing = vectors[..., halfway:]
    return jnp.concatenate(
        [leading * cosine - trailing * sine_part, trailing * cosine + leading * sine_part], axis=-1
    )


def doc_layout(seq_lengths, row_ids):
    ending = jnp.cumsum(seq_lengths, dtype=jnp.int32)
    passed = (ending[None, :] <= row_ids[:, None]).astype(jnp.int32)
    doc_ids = jnp.sum(passed, axis=1, dtype=jnp.int32)
    starting = jnp.sum(passed * seq_lengths[None, :], axis=1, dtype=jnp.int32)
    return (doc_ids, row_ids - starting)


def owner_table(placing):
    slot_range = jnp.arange(placing.shape[0], dtype=jnp.int32)
    return jnp.sum(
        jnp.where(placing[:, None] == slot_range[None, :], slot_range[:, None], 0),
        axis=0,
        dtype=jnp.int32,
    )


def attend(queries, key_all, value_all, allowed):
    score_scale = queries.shape[-1] ** (-0.5)
    scores = (
        jnp.einsum("qhd,khd->hqk", queries, key_all, preferred_element_type=jnp.float32)
        * score_scale
    )
    scores = jnp.where(allowed[None], scores, masked_score)
    largest = jnp.max(scores, axis=2, keepdims=True)
    weights = jnp.where(allowed[None], jnp.exp(scores - largest), 0.0)
    totals = jnp.sum(weights, axis=2)
    summed = jnp.einsum(
        "hqk,khd->hqd",
        weights.astype(jnp.bfloat16),
        value_all,
        preferred_element_type=jnp.float32,
    )
    return (summed / totals[:, :, None]).astype(jnp.bfloat16)


def from_xor(value, distance):
    count = lax.axis_size("seq")
    return lax.ppermute(value, "seq", [(i, i ^ distance) for i in range(count)])


def gather_xor(value):
    count = lax.axis_size("seq")
    even = [value] + [from_xor(value, k) for k in range(2, count, 2)]
    even = jnp.stack(even)
    odd = from_xor(even, 1)
    return jnp.stack([even, odd], axis=1).reshape((count,) + value.shape)


def reduce_xor(parts):
    count = lax.axis_size("seq")
    pairs = parts.reshape((count // 2, 2) + parts.shape[1:])
    got = from_xor(pairs[:, 1], 1)
    both = pairs[:, 0].astype(jnp.float32) + got.astype(jnp.float32)
    total = both[0]
    sent = both[1:].astype(jnp.bfloat16)
    for k in range(1, count // 2):
        total = total + from_xor(sent[k - 1], 2 * k).astype(jnp.float32)
    return total


def move_by_exchange(gate_up, w_down, source_slot):
    slot_index = lax.axis_index("exp")
    slots = lax.axis_size("exp")
    steps = 9
    slot_range = jnp.arange(slots, dtype=jnp.int32)
    dest = owner_table(source_slot)
    crossed = (dest[0] >= 2) & (dest[1] >= 2)
    swapped = jnp.array([0, 2, 1, 3], jnp.int32)
    middle = jnp.where(crossed, swapped, slot_range)
    source_first = jnp.sum(
        jnp.where(middle[:, None] == slot_range[None, :], source_slot[None, :], 0), axis=1
    )
    dest_first = owner_table(source_first)
    own_dest = jnp.sum(jnp.where(slot_range == slot_index, dest_first, 0))
    own_source = jnp.sum(jnp.where(slot_range == slot_index, source_first, 0))
    gate_rows = jnp.swapaxes(gate_up, 2, 3)
    gate = gate_rows.reshape(2, steps, gate_rows.shape[2] // steps, gate_rows.shape[3])
    down = w_down.reshape(steps, w_down.shape[1] // steps, w_down.shape[2])
    gate_new, down_new = gate, down
    upward = [(i, i + 1) for i in range(slots - 1)]
    downward = [(i + 1, i) for i in range(slots - 1)]
    above = slots - 1 - slot_index
    use_up = own_source < slot_index
    moved = own_source != slot_index
    gate_got = down_got = None

    def pick(gate_part, down_part, at):
        at = jnp.clip(at, 0, steps - 1)
        return (
            lax.dynamic_index_in_dim(gate_part, at, 1, keepdims=False),
            lax.dynamic_index_in_dim(down_part, at, 0, keepdims=False),
        )

    got_up = got_down = None
    for step in range(steps + slots - 2):
        up = pick(gate, down, step - slot_index)
        low = pick(gate, down, step - above)
        if got_up is not None:
            up = tuple(jnp.where(own_dest > slot_index, a, b) for a, b in zip(up, got_up))
            low = tuple(jnp.where(own_dest < slot_index, a, b) for a, b in zip(low, got_down))
        got_up = tuple(lax.ppermute(a, "exp", upward) for a in up)
        got_down = tuple(lax.ppermute(a, "exp", downward) for a in low)
        at = jnp.where(use_up, step - slot_index + 1, step - above + 1)
        keep = moved & (at >= 0) & (at < steps)
        at = jnp.clip(at, 0, steps - 1)
        old = pick(gate_new, down_new, at)
        fresh = tuple(
            jnp.where(keep, jnp.where(use_up, a, b), c)
            for a, b, c in zip(got_up, got_down, old)
        )
        gate_new = lax.dynamic_update_index_in_dim(gate_new, fresh[0], at, 1)
        down_new = lax.dynamic_update_index_in_dim(down_new, fresh[1], at, 0)

    def swap_middle(held):
        other = [lax.ppermute(a, "exp", [(1, 2), (2, 1)]) for a in held]
        inner = (slot_index == 1) | (slot_index == 2)
        return tuple(jnp.where(inner, a, b) for a, b in zip(other, held))

    gate_new, down_new = lax.cond(crossed, swap_middle, lambda held: held, (gate_new, down_new))
    gate_new = jnp.swapaxes(gate_new.reshape(gate_rows.shape), 2, 3)
    return gate_new, down_new.reshape(w_down.shape)


def move_by_scatter(gate_up, w_down, source_slot):
    exp_count = lax.axis_size("exp")
    model_width, slice_width = gate_up.shape[2:]
    piece_width = model_width // exp_count
    gate_split = gate_up.reshape(2, exp_count, piece_width, slice_width)
    down_split = w_down.reshape(slice_width, exp_count, piece_width)
    gate_held = lax.all_to_all(gate_split, "exp", split_axis=1, concat_axis=1, tiled=True)
    down_held = lax.all_to_all(down_split, "exp", split_axis=1, concat_axis=1, tiled=True)
    gate_sorted = jnp.take(gate_held, source_slot, axis=1)
    down_sorted = jnp.take(down_held, source_slot, axis=1)
    gate_moved = lax.all_to_all(gate_sorted, "exp", split_axis=1, concat_axis=1, tiled=True)
    down_moved = lax.all_to_all(down_sorted, "exp", split_axis=1, concat_axis=1, tiled=True)
    return gate_moved.reshape(gate_up.shape), down_moved.reshape(w_down.shape)


def shards(
    tokens,
    norm_gain,
    w_qkv,
    w_out,
    moe_gain,
    w_router,
    gate_up,
    w_down,
    lengths,
    blocks_seen,
    expert_ids,
    old_place,
    new_place,
):
    block_rows = tokens.shape[0]
    model_width = tokens.shape[1]
    exp_count = lax.axis_size("exp")
    seq_count = lax.axis_size("seq")
    block_index = lax.axis_index("seq")
    slot_index = lax.axis_index("exp")
    expert_range = jnp.arange(w_router.shape[1], dtype=jnp.int32)

    slot_old = owner_table(old_place)
    source_slot = jnp.sum(
        jnp.where(new_place[:, None] == expert_range[None, :], slot_old[None, :], 0),
        axis=1,
        dtype=jnp.int32,
    )
    movable = exp_count == 4 and w_down.shape[1] % 9 == 0
    move = move_by_exchange if movable else move_by_scatter
    new_gate_up, new_down = move(gate_up, w_down, source_slot)

    ids_all = lax.all_gather(expert_ids, ("seq", "exp"), axis=0, tiled=True)
    heads_here = w_qkv.shape[2] // HEAD_DIM
    query_rows = block_index * block_rows + jnp.arange(block_rows, dtype=jnp.int32)
    query_docs, query_places = doc_layout(lengths, query_rows)
    normed = rms_scale(tokens, norm_gain).astype(jnp.bfloat16)
    projected = [
        jnp.dot(normed, w_qkv[:, part], preferred_element_type=jnp.float32).reshape(
            block_rows, heads_here, HEAD_DIM
        )
        for part in range(3)
    ]
    angle_rows = query_places.astype(jnp.float32)
    queries = rotate(projected[0], angle_rows).astype(jnp.bfloat16)
    key_block = rotate(projected[1], angle_rows).astype(jnp.bfloat16)
    value_block = projected[2].astype(jnp.bfloat16)
    pair = jnp.concatenate(
        [key_block.reshape(block_rows, -1), value_block.reshape(block_rows, -1)], axis=1
    )
    pair_all = gather_xor(pair).reshape(seq_count * block_rows, 2, heads_here, HEAD_DIM)
    order = block_index ^ jnp.arange(seq_count, dtype=jnp.int32)
    key_rows = (
        order[:, None] * block_rows + jnp.arange(block_rows, dtype=jnp.int32)[None, :]
    ).reshape(-1)
    key_docs, _ = doc_layout(lengths, key_rows)
    seen = jnp.take(blocks_seen[0], order)
    key_seen = jnp.repeat(seen, block_rows) == 1
    allowed = (
        (query_docs[:, None] == key_docs[None, :])
        & (key_rows[None, :] <= query_rows[:, None])
        & key_seen[None, :]
    )
    attended = attend(queries, pair_all[:, 0], pair_all[:, 1], allowed)
    attended = jnp.transpose(attended, (1, 0, 2)).reshape(block_rows, heads_here * HEAD_DIM)
    shard_rows = block_rows // exp_count
    partial = jnp.dot(attended, w_out, preferred_element_type=jnp.float32).astype(jnp.bfloat16)
    partials = lax.all_to_all(
        partial.reshape(exp_count, shard_rows, model_width), "exp", 0, 0, tiled=True
    )
    head_total = jnp.sum(partials.astype(jnp.float32), axis=0)
    residual = lax.dynamic_slice_in_dim(tokens, slot_index * shard_rows, shard_rows, 0)
    hidden = (residual.astype(jnp.float32) + head_total).astype(jnp.bfloat16)
    moe_in = rms_scale(hidden, moe_gain).astype(jnp.bfloat16)
    spread = jnp.broadcast_to(moe_in[None], (exp_count,) + moe_in.shape)
    block_in = lax.all_to_all(spread, "exp", 0, 0, tiled=True)
    flat_rows = gather_xor(block_in.reshape(block_rows, model_width)).reshape(-1, model_width)

    ids = jnp.take(ids_all.reshape(seq_count, block_rows, 2), order, axis=0).reshape(-1, 2)
    logits = jnp.dot(flat_rows, w_router, preferred_element_type=jnp.float32)
    chosen = jnp.sum(
        jnp.where(ids[:, :, None] == expert_range[None, None, :], logits[:, None, :], 0.0),
        axis=2,
    )
    gate_first = 1.0 / (1.0 + jnp.exp(chosen[:, 1] - chosen[:, 0]))
    gate_second = 1.0 / (1.0 + jnp.exp(chosen[:, 0] - chosen[:, 1]))
    here = jnp.sum(jnp.where(expert_range == slot_index, old_place, 0))
    gating = jnp.where(
        ids[:, 0] == here, gate_first, jnp.where(ids[:, 1] == here, gate_second, 0.0)
    )
    projected_gate = jnp.dot(flat_rows, gate_up[0, 0], preferred_element_type=jnp.float32)
    projected_up = jnp.dot(flat_rows, gate_up[0, 1], preferred_element_type=jnp.float32)
    activated = (jax.nn.silu(projected_gate) * projected_up).astype(jnp.bfloat16)
    flat_out = jnp.dot(activated, w_down[0], preferred_element_type=jnp.float32)
    weighted = (flat_out * gating[:, None]).astype(jnp.bfloat16)
    summed = reduce_xor(weighted.reshape(seq_count, block_rows, model_width))
    returned = lax.all_to_all(
        summed.astype(jnp.bfloat16).reshape(exp_count, shard_rows, model_width),
        "exp",
        0,
        0,
        tiled=True,
    )
    moe_sum = jnp.sum(returned.astype(jnp.float32), axis=0)
    layer_out = (hidden.astype(jnp.float32) + moe_sum).astype(jnp.bfloat16)
    return (layer_out, new_gate_up, new_down)


def solution(mesh):
    in_specs = (
        P("seq", None),
        P(),
        P(None, None, "exp"),
        P("exp", None),
        P(),
        P(),
        P("exp", None, None, "seq"),
        P("exp", "seq", None),
        P(),
        P("seq", None),
        P(("seq", "exp"), None),
        P(),
        P(),
    )
    out_specs = (P(("seq", "exp"), None), P("exp", None, None, "seq"), P("exp", "seq", None))
    return jax.shard_map(shards, mesh=mesh, in_specs=in_specs, out_specs=out_specs, check_vma=False)
```

time: 707 us -> 553 us (0.78); the launches traced: 706 us -> 544 us
  waiting for transfers between devices: 541 us -> 88.1 us
  starting transfers between devices: 28.7 us -> 172 us
  other arithmetic: 18.6 us -> 101 us
  blocking collectives: 0 us -> 74.7 us
  between operations: 14.8 us -> 6.31 us
    all_to_all x6 -> x3, waiting for transfers between devices: 416 us -> 12.5 us  [the longest x1 12.5 us: shards(): lax.all_to_all(summed.astype(jnp.bfloat16).reshape(exp_count, shard_rows,...]
    ppermute x0 -> x56, starting transfers between devices: none -> 157 us  [the longest x22 117 us: move_by_exchange(): got_up = tuple((lax.ppermute(a, 'exp', upward) for a in up))]
    ppermute x0 -> x56, waiting for transfers between devices: none -> 75.6 us  [the longest x22 42 us: move_by_exchange(): got_down = tuple((lax.ppermute(a, 'exp', downward) for a in low))]
    all_gather x0 -> x1, blocking collectives: none -> 74.7 us  [shards(): ids_all = lax.all_gather(expert_ids, ('seq', 'exp'), axis=0, tiled=True)]
    reduce_scatter x2 -> x0, waiting for transfers between devices: 74.4 us -> none  [the longest x1 53.1 us: shards(): lax.psum_scatter(flat_out.reshape(source_count * lax.axis_size('seq'), it...]
    all_gather x3 -> x0, waiting for transfers between devices: 50 us -> none  [the longest x1 26.1 us: shards(): lax.all_gather(value_block, 'seq', axis=0, tiled=True)]
    select_n x4 -> x24, other arithmetic: 10.9 us -> 47.9 us  [the longest x20 47.3 us: move_by_exchange(): jnp.where(own_dest < slot_index, a, b)]
    dynamic_update_slice x0 -> x22, other arithmetic: none -> 35.2 us  [the longest x11 18.1 us: move_by_exchange(): down_new = lax.dynamic_update_index_in_dim(down_new, fresh[1], at, 0)]
  transfers between devices with their start and end apart: 11 -> 59, of which waited for: 8 -> 16; matrix products, arithmetic and copies ran while one was open for 12% -> 30% of each run, Pallas kernels for 0% -> 0%
where the time goes in v1:
time: 553 us; the launch traced here: 544 us
  starting transfers between devices  172 us (31%)
  other arithmetic  101 us (18%)
  waiting for transfers between devices  88.1 us (16%)
  blocking collectives  74.7 us (14%)
  local copies, waits for them, and re-layouts  67 us (12%)
  matrix products  34.9 us (6%)
  between operations  6.31 us (1%)
    ppermute x22, starting transfers between devices, move_by_exchange(): got_up = tuple((lax.ppermute(a, 'exp', upward) for a in up))  117 us
    all_gather x1, blocking collectives, shards(): ids_all = lax.all_gather(expert_ids, ('seq', 'exp'), axis=0, tiled=True)  74.7 us
    select_n x20, other arithmetic, move_by_exchange(): jnp.where(own_dest < slot_index, a, b)  47.3 us
    ppermute x22, waiting for transfers between devices, move_by_exchange(): got_down = tuple((lax.ppermute(a, 'exp', downward) for a in low))  42 us
    ppermute x12, waiting for transfers between devices, from_xor(): return lax.ppermute(value, 'seq', [(i, i ^ distance) for i in range(count)])  29.3 us
    ppermute x22, starting transfers between devices, move_by_exchange(): got_down = tuple((lax.ppermute(a, 'exp', downward) for a in low))  28.2 us
    dot_general x4, local copies, waits for them, and re-layouts, shards(): jnp.dot(normed, w_qkv[:, part], preferred_element_type=jnp.float32)  19.2 us
    dynamic_update_slice x11, other arithmetic, move_by_exchange(): down_new = lax.dynamic_update_index_in_dim(down_new, fresh[1], at, 0)  18.1 us
  transfers between devices with their start and end apart: 59, of which 16 were waited for; matrix products, arithmetic and copies ran while one was open for 30% of the time, Pallas kernels for 0%

profile of v1, /device:TPU:0, one launch (start us, length us, event | category | flops | bytes accessed | tf_op | source)
XLA Modules:
  0.0 544.1 jit_solution(9839655124325824131)
XLA Ops:
  8.7 6.1 %slice_bitcast_fusion.4 = (bf16[512,2304]{0,1:T(8,128)(2,1)}, bf16[512,2304]{0,1:T(8,128)(2,1)}, bf16[512,2304]{0,1:T(8,128)(2,1)}) fusion(bf16[2304,3,512]{2,0,1:T(8,128)(2,1)} %param.18), kind=kLoop, calls=%fused_computation.25 | loop fusion | bytes 14155776 | tf_op jit(solution)/shard_map/dot_general | solution.py:211
  48.7 5.3 collective-permute-start.36
  64.2 5.6 %collective-permute-start.38 = (bf16[80,2304]{1,0:T(8,128)(2,1)}, bf16[80,2304]{1,0:T(8,128)(2,1)}, u32[]{:S(2)}, u32[]{:S(2)}) collective-permute-start(bf16[80,2304]{1,0:T(8,128)(2,1)} %get-tuple-element.84), channel_id=1, source_target_pairs={{0,1},{1,2},{2,3},{4,5},{5,6},{6,7},{8,9},{9,10},{10,11},{12,13},{... | collective-permute-start | bytes 1105928 | tf_op jit(solution)/shard_map/ppermute | solution.py:134
  72.0 4.6 collective-permute-start.14
  80.8 4.6 collective-permute-start.40
  85.3 6.9 %collective-permute-done.15 = bf16[2,80,2304]{2,1,0:T(8,128)(2,1)S(1)} collective-permute-done((bf16[2,80,2304]{2,1,0:T(8,128)(2,1)}, bf16[2,80,2304]{2,1,0:T(8,128)(2,1)S(1)}, u32[]{:S(2)}, u32[]{:S(2)}) %collective-permute-start.15) | collective-permute-done | bytes 737312 | tf_op jit(solution)/shard_map/ppermute | solution.py:135
  98.0 5.8 %collective-permute-start.16 = (bf16[2,80,2304]{2,1,0:T(8,128)(2,1)}, bf16[2,80,2304]{2,1,0:T(8,128)(2,1)}, u32[]{:S(2)}, u32[]{:S(2)}) collective-permute-start(bf16[2,80,2304]{2,1,0:T(8,128)(2,1)} %get-tuple-element.61), channel_id=1, source_target_pairs={{0,1},{1,2},{2,3},{4,5},{5,6},{6,7},{8,9},{9,10},{10,11},{12,13},{... | collective-permute-start | bytes 2211848 | tf_op jit(solution)/shard_map/ppermute | solution.py:134
  107.5 5.5 %collective-permute-start.42 = (bf16[80,2304]{1,0:T(8,128)(2,1)}, bf16[80,2304]{1,0:T(8,128)(2,1)}, u32[]{:S(2)}, u32[]{:S(2)}) collective-permute-start(bf16[80,2304]{1,0:T(8,128)(2,1)} %get-tuple-element.80), channel_id=1, source_target_pairs={{0,1},{1,2},{2,3},{4,5},{5,6},{6,7},{8,9},{9,10},{10,11},{12,13},{... | collective-permute-start | bytes 1105928 | tf_op jit(solution)/shard_map/ppermute | solution.py:134
  134.7 4.6 collective-permute-start.44
  143.6 4.6 collective-permute-start.18
  153.7 7.8 %collective-permute-start.46 = (bf16[80,2304]{1,0:T(8,128)(2,1)}, bf16[80,2304]{1,0:T(8,128)(2,1)}, u32[]{:S(2)}, u32[]{:S(2)}) collective-permute-start(bf16[80,2304]{1,0:T(8,128)(2,1)} %get-tuple-element.76), channel_id=1, source_target_pairs={{0,1},{1,2},{2,3},{4,5},{5,6},{6,7},{8,9},{9,10},{10,11},{12,13},{... | collective-permute-start | bytes 1105928 | tf_op jit(solution)/shard_map/ppermute | solution.py:134
  169.2 7.1 %collective-permute-start.20 = (bf16[2,80,2304]{2,1,0:T(8,128)(2,1)S(1)}, bf16[2,80,2304]{2,1,0:T(8,128)(2,1)S(1)}, u32[]{:S(2)}, u32[]{:S(2)}) collective-permute-start(bf16[2,80,2304]{2,1,0:T(8,128)(2,1)S(1)} %get-tuple-element.57), channel_id=1, source_target_pairs={{0,1},{1,2},{2,3},{4,5},{5,6},{6,7},{8,9},{9,10},{10,11},{12,13},{... | collective-permute-start | bytes 2211848 | tf_op jit(solution)/shard_map/ppermute | solution.py:134
  179.9 5.3 collective-permute-start.48
  193.8 7.1 %collective-permute-start.22 = (bf16[2,80,2304]{2,1,0:T(8,128)(2,1)}, bf16[2,80,2304]{2,1,0:T(8,128)(2,1)S(1)}, u32[]{:S(2)}, u32[]{:S(2)}) collective-permute-start(bf16[2,80,2304]{2,1,0:T(8,128)(2,1)} %get-tuple-element.55), channel_id=1, source_target_pairs={{0,1},{1,2},{2,3},{4,5},{5,6},{6,7},{8,9},{9,10},{10,11},{12,13},{... | collective-permute-start | bytes 2211848 | tf_op jit(solution)/shard_map/ppermute | solution.py:134
  209.6 5.3 collective-permute-start.50
  214.9 5.0 collective-permute-done.23
  224.3 7.5 %collective-permute-start.24 = (bf16[2,80,2304]{2,1,0:T(8,128)(2,1)}, bf16[2,80,2304]{2,1,0:T(8,128)(2,1)}, u32[]{:S(2)}, u32[]{:S(2)}) collective-permute-start(bf16[2,80,2304]{2,1,0:T(8,128)(2,1)} %get-tuple-element.53), channel_id=1, source_target_pairs={{0,1},{1,2},{2,3},{4,5},{5,6},{6,7},{8,9},{9,10},{10,11},{12,13},{... | collective-permute-start | bytes 2211848 | tf_op jit(solution)/shard_map/ppermute | solution.py:134
  231.9 74.7 %all-gather = s32[32,32,2]{1,2,0:T(2,128)S(1)} all-gather(s32[1,32,2]{1,2,0:T(2,128)S(1)} %bitcast.398), channel_id=1, replica_groups=mesh['seq'=8,'exp'=4] {'seq','exp'}, dimensions={0}, use_global_device_ids=true | all-gather | bytes 8448 | tf_op jit(solution)/shard_map/all_gather | solution.py:205
  310.8 5.3 collective-permute-start.52
  322.6 4.6 collective-permute-start.26
  349.6 5.4 collective-permute-start.28
  362.2 7.6 %collective-permute-done.29 = bf16[2,80,2304]{2,1,0:T(8,128)(2,1)} collective-permute-done((bf16[2,80,2304]{2,1,0:T(8,128)(2,1)}, bf16[2,80,2304]{2,1,0:T(8,128)(2,1)}, u32[]{:S(2)}, u32[]{:S(2)}) %collective-permute-start.29) | collective-permute-done | bytes 737312 | tf_op jit(solution)/shard_map/ppermute | solution.py:135
  375.7 5.7 %collective-permute-start.30 = (bf16[2,80,2304]{2,1,0:T(8,128)(2,1)}, bf16[2,80,2304]{2,1,0:T(8,128)(2,1)}, u32[]{:S(2)}, u32[]{:S(2)}) collective-permute-start(bf16[2,80,2304]{2,1,0:T(8,128)(2,1)} %get-tuple-element.47), channel_id=1, source_target_pairs={{0,1},{1,2},{2,3},{4,5},{5,6},{6,7},{8,9},{9,10},{10,11},{12,13},{... | collective-permute-start | bytes 2211848 | tf_op jit(solution)/shard_map/ppermute | solution.py:134
  383.5 9.0 %fusion.4 = f32[1024,720]{0,1:T(8,128)} fusion(bf16[1024,2304]{1,0:T(8,128)(2,1)S(1)} %bitcast.378, bf16[1,2,2304,720]{2,3,1,0:T(8,128)(2,1)} %copy.141), kind=kOutput, calls=%fused_computation.14 | convolution fusion | flops 3397386240 | bytes 10985472 | tf_op jit(solution)/shard_map/dot_general | solution.py:263
  394.5 13.7 %multiply_convert_fusion = bf16[1024,2304]{1,0:T(8,128)(2,1)} fusion(f32[1024]{0:T(1024)S(1)} %bitcast.395, bf16[1,720,2304]{2,1,0:T(8,128)(2,1)} %copy.142, f32[1024,720]{0,1:T(8,128)} %fusion.4, bf16[1024,2304]{1,0:T(8,128)(2,1)} %bitcast.380, bf16[1,2,2304,720]{2,3,1,0:T(8,128)(2,1)} %copy.141), kind=kOutput, calls=%fused_computation.5 | convolution fusion | flops 6803914752 | bytes 19025920 | tf_op jit(solution)/shard_map/dot_general | solution.py:266
  439.9 4.8 collective-permute-start.32
  445.0 12.2 %collective-permute-done.33 = bf16[2,80,2304]{2,1,0:T(8,128)(2,1)S(1)} collective-permute-done((bf16[2,80,2304]{2,1,0:T(8,128)(2,1)S(1)}, bf16[2,80,2304]{2,1,0:T(8,128)(2,1)S(1)}, u32[]{:S(2)}, u32[]{:S(2)}) %collective-permute-start.33) | collective-permute-done | bytes 737312 | tf_op jit(solution)/shard_map/ppermute | solution.py:135
  479.0 5.3 collective-permute-start.34
  497.9 12.5 %collective-permute-done.13 = bf16[128,2304]{1,0:T(8,128)(2,1)S(1)} collective-permute-done((bf16[128,2304]{1,0:T(8,128)(2,1)S(1)}, bf16[128,2304]{1,0:T(8,128)(2,1)S(1)}, u32[]{:S(2)}, u32[]{:S(2)}) %collective-permute-start.13) | collective-permute-done | bytes 589856 | tf_op jit(solution)/shard_map/ppermute | solution.py:71
  510.5 8.5 %collective-permute-done.12 = bf16[128,2304]{1,0:T(8,128)(2,1)S(1)} collective-permute-done((bf16[128,2304]{1,0:T(8,128)(2,1)S(1)}, bf16[128,2304]{1,0:T(8,128)(2,1)S(1)}, u32[]{:S(2)}, u32[]{:S(2)}) %collective-permute-start.12) | collective-permute-done | bytes 589856 | tf_op jit(solution)/shard_map/ppermute | solution.py:71
  520.1 6.7 %all-to-all-start.2 = ((bf16[4,32,2304]{2,1,0:T(8,128)(2,1)}), bf16[4,32,2304]{2,1,0:T(8,128)(2,1)S(1)}, u32[]{:S(2)}, u32[]{:S(2)}) async-start(bf16[4,32,2304]{2,1,0:T(8,128)(2,1)} %bitcast.55), calls=%async_computation.2 | async-start | bytes 1179648 | tf_op jit(solution)/shard_map/all_to_all | solution.py:269
  530.3 12.5 %all-to-all-done.2 = bf16[4,32,2304]{2,1,0:T(8,128)(2,1)S(1)} async-done(((bf16[4,32,2304]{2,1,0:T(8,128)(2,1)}), bf16[4,32,2304]{2,1,0:T(8,128)(2,1)S(1)}, u32[]{:S(2)}, u32[]{:S(2)}) %all-to-all-start.2) | async-done | bytes 589856 | tf_op jit(solution)/shard_map/all_to_all | solution.py:269
  (337 shorter events, 250.4 us)
Async XLA Ops:
  36.9 33.8 %collective-permute-start.4 = (bf16[128,1024]{0,1:T(8,128)(2,1)}, bf16[128,1024]{0,1:T(8,128)(2,1)}, u32[]{:S(2)}, u32[]{:S(2)}) collective-permute-start(bf16[128,1024]{0,1:T(8,128)(2,1)} %get-tuple-element.100), channel_id=1, source_target_pairs={{0,24},{4,28},{8,16},{12,20},{16,8},{20,12},{24,0},{28,4},{1,25},{... | collective-permute-start | bytes 786440 | tf_op jit(solution)/shard_map/ppermute | solution.py:71
  40.8 31.2 %collective-permute-start.3 = (bf16[128,1024]{0,1:T(8,128)(2,1)}, bf16[128,1024]{0,1:T(8,128)(2,1)}, u32[]{:S(2)}, u32[]{:S(2)}) collective-permute-start(bf16[128,1024]{0,1:T(8,128)(2,1)} %get-tuple-element.100), channel_id=1, source_target_pairs={{0,16},{4,20},{8,24},{12,28},{16,0},{20,4},{24,8},{28,12},{1,17},{... | collective-permute-start | bytes 786440 | tf_op jit(solution)/shard_map/ppermute | solution.py:71
  41.3 35.3 %collective-permute-start.2 = (bf16[128,1024]{0,1:T(8,128)(2,1)}, bf16[128,1024]{0,1:T(8,128)(2,1)}, u32[]{:S(2)}, u32[]{:S(2)}) collective-permute-start(bf16[128,1024]{0,1:T(8,128)(2,1)} %get-tuple-element.100), channel_id=1, source_target_pairs={{0,8},{4,12},{8,0},{12,4},{16,24},{20,28},{24,16},{28,20},{1,9},{5... | collective-permute-start | bytes 786440 | tf_op jit(solution)/shard_map/ppermute | solution.py:71
  78.0 35.0 %collective-permute-start.5 = (bf16[4,128,1024]{1,2,0:T(8,128)(2,1)S(1)}, bf16[4,128,1024]{1,2,0:T(8,128)(2,1)S(1)}, u32[]{:S(2)}, u32[]{:S(2)}) collective-permute-start(bf16[4,128,1024]{1,2,0:T(8,128)(2,1)S(1)} %get-tuple-element.94), channel_id=1, source_target_pairs={{0,4},{4,0},{8,12},{12,8},{16,20},{20,16},{24,28},{28,24},{1,5},{5... | collective-permute-start | bytes 3145736 | tf_op jit(solution)/shard_map/ppermute | solution.py:71
  79.5 24.4 %collective-permute-start.41 = (bf16[80,2304]{1,0:T(8,128)(2,1)S(1)}, bf16[80,2304]{1,0:T(8,128)(2,1)S(1)}, u32[]{:S(2)}, u32[]{:S(2)}) collective-permute-start(bf16[80,2304]{1,0:T(8,128)(2,1)S(1)} %get-tuple-element.81), channel_id=1, source_target_pairs={{1,0},{2,1},{3,2},{5,4},{6,5},{7,6},{9,8},{10,9},{11,10},{13,12},{... | collective-permute-start | bytes 1105928 | tf_op jit(solution)/shard_map/ppermute | solution.py:135
  96.7 42.5 %collective-permute-start.17 = (bf16[2,80,2304]{2,1,0:T(8,128)(2,1)}, bf16[2,80,2304]{2,1,0:T(8,128)(2,1)}, u32[]{:S(2)}, u32[]{:S(2)}) collective-permute-start(bf16[2,80,2304]{2,1,0:T(8,128)(2,1)} %get-tuple-element.60), channel_id=1, source_target_pairs={{1,0},{2,1},{3,2},{5,4},{6,5},{7,6},{9,8},{10,9},{11,10},{13,12},{... | collective-permute-start | bytes 2211848 | tf_op jit(solution)/shard_map/ppermute | solution.py:135
  98.0 41.2 %collective-permute-start.16 = (bf16[2,80,2304]{2,1,0:T(8,128)(2,1)}, bf16[2,80,2304]{2,1,0:T(8,128)(2,1)}, u32[]{:S(2)}, u32[]{:S(2)}) collective-permute-start(bf16[2,80,2304]{2,1,0:T(8,128)(2,1)} %get-tuple-element.61), channel_id=1, source_target_pairs={{0,1},{1,2},{2,3},{4,5},{5,6},{6,7},{8,9},{9,10},{10,11},{12,13},{... | collective-permute-start | bytes 2211848 | tf_op jit(solution)/shard_map/ppermute | solution.py:134
  106.2 25.7 %collective-permute-start.43 = (bf16[80,2304]{1,0:T(8,128)(2,1)}, bf16[80,2304]{1,0:T(8,128)(2,1)}, u32[]{:S(2)}, u32[]{:S(2)}) collective-permute-start(bf16[80,2304]{1,0:T(8,128)(2,1)} %get-tuple-element.79), channel_id=1, source_target_pairs={{1,0},{2,1},{3,2},{5,4},{6,5},{7,6},{9,8},{10,9},{11,10},{13,12},{... | collective-permute-start | bytes 1105928 | tf_op jit(solution)/shard_map/ppermute | solution.py:135
  107.5 24.5 %collective-permute-start.42 = (bf16[80,2304]{1,0:T(8,128)(2,1)}, bf16[80,2304]{1,0:T(8,128)(2,1)}, u32[]{:S(2)}, u32[]{:S(2)}) collective-permute-start(bf16[80,2304]{1,0:T(8,128)(2,1)} %get-tuple-element.80), channel_id=1, source_target_pairs={{0,1},{1,2},{2,3},{4,5},{5,6},{6,7},{8,9},{9,10},{10,11},{12,13},{... | collective-permute-start | bytes 1105928 | tf_op jit(solution)/shard_map/ppermute | solution.py:134
  127.4 34.1 %all-to-all-start = ((bf16[4,32,2304]{2,1,0:T(8,128)(2,1)}), bf16[4,32,2304]{2,1,0:T(8,128)(2,1)S(1)}, u32[]{:S(2)}, u32[]{:S(2)}) async-start(bf16[4,32,2304]{2,1,0:T(8,128)(2,1)} %bitcast.31), calls=%async_computation | async-start | bytes 1179648 | tf_op jit(solution)/shard_map/all_to_all | solution.py:240
  142.3 23.5 %collective-permute-start.19 = (bf16[2,80,2304]{2,1,0:T(8,128)(2,1)}, bf16[2,80,2304]{2,1,0:T(8,128)(2,1)S(1)}, u32[]{:S(2)}, u32[]{:S(2)}) collective-permute-start(bf16[2,80,2304]{2,1,0:T(8,128)(2,1)} %get-tuple-element.58), channel_id=1, source_target_pairs={{1,0},{2,1},{3,2},{5,4},{6,5},{7,6},{9,8},{10,9},{11,10},{13,12},{... | collective-permute-start | bytes 2211848 | tf_op jit(solution)/shard_map/ppermute | solution.py:135
  152.4 23.9 %collective-permute-start.47 = (bf16[80,2304]{1,0:T(8,128)(2,1)}, bf16[80,2304]{1,0:T(8,128)(2,1)}, u32[]{:S(2)}, u32[]{:S(2)}) collective-permute-start(bf16[80,2304]{1,0:T(8,128)(2,1)} %get-tuple-element.75), channel_id=1, source_target_pairs={{1,0},{2,1},{3,2},{5,4},{6,5},{7,6},{9,8},{10,9},{11,10},{13,12},{... | collective-permute-start | bytes 1105928 | tf_op jit(solution)/shard_map/ppermute | solution.py:135
  178.6 27.4 %collective-permute-start.49 = (bf16[80,2304]{1,0:T(8,128)(2,1)}, bf16[80,2304]{1,0:T(8,128)(2,1)}, u32[]{:S(2)}, u32[]{:S(2)}) collective-permute-start(bf16[80,2304]{1,0:T(8,128)(2,1)} %get-tuple-element.73), channel_id=1, source_target_pairs={{1,0},{2,1},{3,2},{5,4},{6,5},{7,6},{9,8},{10,9},{11,10},{13,12},{... | collective-permute-start | bytes 1105928 | tf_op jit(solution)/shard_map/ppermute | solution.py:135
  179.9 26.1 %collective-permute-start.48 = (bf16[80,2304]{1,0:T(8,128)(2,1)}, bf16[80,2304]{1,0:T(8,128)(2,1)}, u32[]{:S(2)}, u32[]{:S(2)}) collective-permute-start(bf16[80,2304]{1,0:T(8,128)(2,1)} %get-tuple-element.74), channel_id=1, source_target_pairs={{0,1},{1,2},{2,3},{4,5},{5,6},{6,7},{8,9},{9,10},{10,11},{12,13},{... | collective-permute-start | bytes 1105928 | tf_op jit(solution)/shard_map/ppermute | solution.py:134
  192.5 27.4 %collective-permute-start.23 = (bf16[2,80,2304]{2,1,0:T(8,128)(2,1)}, bf16[2,80,2304]{2,1,0:T(8,128)(2,1)S(1)}, u32[]{:S(2)}, u32[]{:S(2)}) collective-permute-start(bf16[2,80,2304]{2,1,0:T(8,128)(2,1)} %get-tuple-element.54), channel_id=1, source_target_pairs={{1,0},{2,1},{3,2},{5,4},{6,5},{7,6},{9,8},{10,9},{11,10},{13,12},{... | collective-permute-start | bytes 2211848 | tf_op jit(solution)/shard_map/ppermute | solution.py:135
  193.8 26.1 %collective-permute-start.22 = (bf16[2,80,2304]{2,1,0:T(8,128)(2,1)}, bf16[2,80,2304]{2,1,0:T(8,128)(2,1)S(1)}, u32[]{:S(2)}, u32[]{:S(2)}) collective-permute-start(bf16[2,80,2304]{2,1,0:T(8,128)(2,1)} %get-tuple-element.55), channel_id=1, source_target_pairs={{0,1},{1,2},{2,3},{4,5},{5,6},{6,7},{8,9},{9,10},{10,11},{12,13},{... | collective-permute-start | bytes 2211848 | tf_op jit(solution)/shard_map/ppermute | solution.py:134
  201.8 114.3 %all-to-all-start.1 = ((bf16[4,32,2304]{2,1,0:T(8,128)(2,1)}), bf16[4,32,2304]{2,1,0:T(8,128)(2,1)}, u32[]{:S(2)}, u32[]{:S(2)}) async-start(bf16[4,32,2304]{2,1,0:T(8,128)(2,1)} %broadcast_in_dim.221), calls=%async_computation.1 | async-start | bytes 1179648 | tf_op jit(solution)/shard_map/all_to_all | solution.py:248
  208.3 99.0 %collective-permute-start.51 = (bf16[80,2304]{1,0:T(8,128)(2,1)}, bf16[80,2304]{1,0:T(8,128)(2,1)}, u32[]{:S(2)}, u32[]{:S(2)}) collective-permute-start(bf16[80,2304]{1,0:T(8,128)(2,1)} %get-tuple-element.71), channel_id=1, source_target_pairs={{1,0},{2,1},{3,2},{5,4},{6,5},{7,6},{9,8},{10,9},{11,10},{13,12},{... | collective-permute-start | bytes 1105928 | tf_op jit(solution)/shard_map/ppermute | solution.py:135
  209.6 97.7 %collective-permute-start.50 = (bf16[80,2304]{1,0:T(8,128)(2,1)}, bf16[80,2304]{1,0:T(8,128)(2,1)}, u32[]{:S(2)}, u32[]{:S(2)}) collective-permute-start(bf16[80,2304]{1,0:T(8,128)(2,1)} %get-tuple-element.72), channel_id=1, source_target_pairs={{0,1},{1,2},{2,3},{4,5},{5,6},{6,7},{8,9},{9,10},{10,11},{12,13},{... | collective-permute-start | bytes 1105928 | tf_op jit(solution)/shard_map/ppermute | solution.py:134
  223.1 93.0 %collective-permute-start.25 = (bf16[2,80,2304]{2,1,0:T(8,128)(2,1)}, bf16[2,80,2304]{2,1,0:T(8,128)(2,1)S(1)}, u32[]{:S(2)}, u32[]{:S(2)}) collective-permute-start(bf16[2,80,2304]{2,1,0:T(8,128)(2,1)} %get-tuple-element.52), channel_id=1, source_target_pairs={{1,0},{2,1},{3,2},{5,4},{6,5},{7,6},{9,8},{10,9},{11,10},{13,12},{... | collective-permute-start | bytes 2211848 | tf_op jit(solution)/shard_map/ppermute | solution.py:135
  224.3 93.3 %collective-permute-start.24 = (bf16[2,80,2304]{2,1,0:T(8,128)(2,1)}, bf16[2,80,2304]{2,1,0:T(8,128)(2,1)}, u32[]{:S(2)}, u32[]{:S(2)}) collective-permute-start(bf16[2,80,2304]{2,1,0:T(8,128)(2,1)} %get-tuple-element.53), channel_id=1, source_target_pairs={{0,1},{1,2},{2,3},{4,5},{5,6},{6,7},{8,9},{9,10},{10,11},{12,13},{... | collective-permute-start | bytes 2211848 | tf_op jit(solution)/shard_map/ppermute | solution.py:134
  317.7 23.7 %collective-permute-start.6 = (bf16[128,2304]{1,0:T(8,128)(2,1)}, bf16[128,2304]{1,0:T(8,128)(2,1)S(1)}, u32[]{:S(2)}, u32[]{:S(2)}) collective-permute-start(bf16[128,2304]{1,0:T(8,128)(2,1)} %bitcast.33), channel_id=1, source_target_pairs={{0,8},{4,12},{8,0},{12,4},{16,24},{20,28},{24,16},{28,20},{1,9},{5... | collective-permute-start | bytes 1769480 | tf_op jit(solution)/shard_map/ppermute | solution.py:71
  321.3 23.4 %collective-permute-start.27 = (bf16[2,80,2304]{2,1,0:T(8,128)(2,1)S(1)}, bf16[2,80,2304]{2,1,0:T(8,128)(2,1)S(1)}, u32[]{:S(2)}, u32[]{:S(2)}) collective-permute-start(bf16[2,80,2304]{2,1,0:T(8,128)(2,1)S(1)} %get-tuple-element.50), channel_id=1, source_target_pairs={{1,0},{2,1},{3,2},{5,4},{6,5},{7,6},{9,8},{10,9},{11,10},{13,12},{... | collective-permute-start | bytes 2211848 | tf_op jit(solution)/shard_map/ppermute | solution.py:135
  344.7 36.7 %collective-permute-start.9 = (bf16[4,128,2304]{2,1,0:T(8,128)(2,1)}, bf16[4,128,2304]{2,1,0:T(8,128)(2,1)}, u32[]{:S(2)}, u32[]{:S(2)}) collective-permute-start(bf16[4,128,2304]{2,1,0:T(8,128)(2,1)} %get-tuple-element.92), channel_id=1, source_target_pairs={{0,4},{4,0},{8,12},{12,8},{16,20},{20,16},{24,28},{28,24},{1,5},{5... | collective-permute-start | bytes 7077896 | tf_op jit(solution)/shard_map/ppermute | solution.py:71
  358.3 76.4 %collective-permute-start.56 = (bf16[80,2304]{1,0:T(8,128)(2,1)}, bf16[80,2304]{1,0:T(8,128)(2,1)}, u32[]{:S(2)}, u32[]{:S(2)}) collective-permute-start(bf16[80,2304]{1,0:T(8,128)(2,1)} %get-tuple-element.66), channel_id=1, source_target_pairs={{0,1},{1,2},{2,3},{4,5},{5,6},{6,7},{8,9},{9,10},{10,11},{12,13},{... | collective-permute-start | bytes 1105928 | tf_op jit(solution)/shard_map/ppermute | solution.py:134
  361.0 73.8 %collective-permute-start.57 = (bf16[80,2304]{1,0:T(8,128)(2,1)}, bf16[80,2304]{1,0:T(8,128)(2,1)}, u32[]{:S(2)}, u32[]{:S(2)}) collective-permute-start(bf16[80,2304]{1,0:T(8,128)(2,1)} %get-tuple-element.65), channel_id=1, source_target_pairs={{1,0},{2,1},{3,2},{5,4},{6,5},{7,6},{9,8},{10,9},{11,10},{13,12},{... | collective-permute-start | bytes 1105928 | tf_op jit(solution)/shard_map/ppermute | solution.py:135
  374.4 62.2 %collective-permute-start.31 = (bf16[2,80,2304]{2,1,0:T(8,128)(2,1)}, bf16[2,80,2304]{2,1,0:T(8,128)(2,1)}, u32[]{:S(2)}, u32[]{:S(2)}) collective-permute-start(bf16[2,80,2304]{2,1,0:T(8,128)(2,1)} %get-tuple-element.46), channel_id=1, source_target_pairs={{1,0},{2,1},{3,2},{5,4},{6,5},{7,6},{9,8},{10,9},{11,10},{13,12},{... | collective-permute-start | bytes 2211848 | tf_op jit(solution)/shard_map/ppermute | solution.py:135
  375.7 60.9 %collective-permute-start.30 = (bf16[2,80,2304]{2,1,0:T(8,128)(2,1)}, bf16[2,80,2304]{2,1,0:T(8,128)(2,1)}, u32[]{:S(2)}, u32[]{:S(2)}) collective-permute-start(bf16[2,80,2304]{2,1,0:T(8,128)(2,1)} %get-tuple-element.47), channel_id=1, source_target_pairs={{0,1},{1,2},{2,3},{4,5},{5,6},{6,7},{8,9},{9,10},{10,11},{12,13},{... | collective-permute-start | bytes 2211848 | tf_op jit(solution)/shard_map/ppermute | solution.py:134
  444.9 47.5 %collective-permute-start.10 = (bf16[4,128,2304]{2,1,0:T(8,128)(2,1)S(1)}, bf16[4,128,2304]{2,1,0:T(8,128)(2,1)S(1)}, u32[]{:S(2)}, u32[]{:S(2)}) collective-permute-start(bf16[4,128,2304]{2,1,0:T(8,128)(2,1)S(1)} %slice_bitcast_fusion), channel_id=1, source_target_pairs={{0,4},{4,0},{8,12},{12,8},{16,20},{20,16},{24,28},{28,24},{1,5},{5... | collective-permute-start | bytes 7077896 | tf_op jit(solution)/shard_map/ppermute | solution.py:71
  479.0 49.0 %collective-permute-start.34 = (bf16[2,80,2304]{2,1,0:T(8,128)(2,1)}, bf16[2,80,2304]{2,1,0:T(8,128)(2,1)}, u32[]{:S(2)}, u32[]{:S(2)}) collective-permute-start(bf16[2,80,2304]{2,1,0:T(8,128)(2,1)} %get-tuple-element.43), channel_id=1, source_target_pairs={{0,1},{1,2},{2,3},{4,5},{5,6},{6,7},{8,9},{9,10},{10,11},{12,13},{... | collective-permute-start | bytes 2211848 | tf_op jit(solution)/shard_map/ppermute | solution.py:134
  484.3 43.7 %collective-permute-start.35 = (bf16[2,80,2304]{2,1,0:T(8,128)(2,1)}, bf16[2,80,2304]{2,1,0:T(8,128)(2,1)}, u32[]{:S(2)}, u32[]{:S(2)}) collective-permute-start(bf16[2,80,2304]{2,1,0:T(8,128)(2,1)} %get-tuple-element.42), channel_id=1, source_target_pairs={{1,0},{2,1},{3,2},{5,4},{6,5},{7,6},{9,8},{10,9},{11,10},{13,12},{... | collective-permute-start | bytes 2211848 | tf_op jit(solution)/shard_map/ppermute | solution.py:135
  494.4 24.5 %collective-permute-start.12 = (bf16[128,2304]{1,0:T(8,128)(2,1)S(1)}, bf16[128,2304]{1,0:T(8,128)(2,1)S(1)}, u32[]{:S(2)}, u32[]{:S(2)}) collective-permute-start(bf16[128,2304]{1,0:T(8,128)(2,1)S(1)} %get-tuple-element.90), channel_id=1, source_target_pairs={{0,16},{4,20},{8,24},{12,28},{16,0},{20,4},{24,8},{28,12},{1,17},{... | collective-permute-start | bytes 1769480 | tf_op jit(solution)/shard_map/ppermute | solution.py:71
  (83 other events, 1354.6 us)

commit v2 on v1

--- a/solution.py
+++ b/solution.py
@@ -1,5 +1,8 @@
+import itertools
+
 import jax
 import jax.numpy as jnp
+import numpy as np
 from jax import lax
 from jax.sharding import PartitionSpec as P
 
@@ -89,69 +92,6 @@
     for k in range(1, count // 2):
         total = total + from_xor(sent[k - 1], 2 * k).astype(jnp.float32)
     return total
-
-
-def move_by_exchange(gate_up, w_down, source_slot):
-    slot_index = lax.axis_index("exp")
-    slots = lax.axis_size("exp")
-    steps = 9
-    slot_range = jnp.arange(slots, dtype=jnp.int32)
-    dest = owner_table(source_slot)
-    crossed = (dest[0] >= 2) & (dest[1] >= 2)
-    swapped = jnp.array([0, 2, 1, 3], jnp.int32)
-    middle = jnp.where(crossed, swapped, slot_range)
-    source_first = jnp.sum(
-        jnp.where(middle[:, None] == slot_range[None, :], source_slot[None, :], 0), axis=1
-    )
-    dest_first = owner_table(source_first)
-    own_dest = jnp.sum(jnp.where(slot_range == slot_index, dest_first, 0))
-    own_source = jnp.sum(jnp.where(slot_range == slot_index, source_first, 0))
-    gate_rows = jnp.swapaxes(gate_up, 2, 3)
-    gate = gate_rows.reshape(2, steps, gate_rows.shape[2] // steps, gate_rows.shape[3])
-    down = w_down.reshape(steps, w_down.shape[1] // steps, w_down.shape[2])
-    gate_new, down_new = gate, down
-    upward = [(i, i + 1) for i in range(slots - 1)]
-    downward = [(i + 1, i) for i in range(slots - 1)]
-    above = slots - 1 - slot_index
-    use_up = own_source < slot_index
-    moved = own_source != slot_index
-    gate_got = down_got = None
-
-    def pick(gate_part, down_part, at):
-        at = jnp.clip(at, 0, steps - 1)
-        return (
-            lax.dynamic_index_in_dim(gate_part, at, 1, keepdims=False),
-            lax.dynamic_index_in_dim(down_part, at, 0, keepdims=False),
-        )
-
-    got_up = got_down = None
-    for step in range(steps + slots - 2):
-        up = pick(gate, down, step - slot_index)
-        low = pick(gate, down, step - above)
-        if got_up is not None:
-            up = tuple(jnp.where(own_dest > slot_index, a, b) for a, b in zip(up, got_up))
-            low = tuple(jnp.where(own_dest < slot_index, a, b) for a, b in zip(low, got_down))
-        got_up = tuple(lax.ppermute(a, "exp", upward) for a in up)
-        got_down = tuple(lax.ppermute(a, "exp", downward) for a in low)
-        at = jnp.where(use_up, step - slot_index + 1, step - above + 1)
-        keep = moved & (at >= 0) & (at < steps)
-        at = jnp.clip(at, 0, steps - 1)
-        old = pick(gate_new, down_new, at)
-        fresh = tuple(
-            jnp.where(keep, jnp.where(use_up, a, b), c)
-            for a, b, c in zip(got_up, got_down, old)
-        )
-        gate_new = lax.dynamic_update_index_in_dim(gate_new, fresh[0], at, 1)
-        down_new = lax.dynamic_update_index_in_dim(down_new, fresh[1], at, 0)
-
-    def swap_middle(held):
-        other = [lax.ppermute(a, "exp", [(1, 2), (2, 1)]) for a in held]
-        inner = (slot_index == 1) | (slot_index == 2)
-        return tuple(jnp.where(inner, a, b) for a, b in zip(other, held))
-
-    gate_new, down_new = lax.cond(crossed, swap_middle, lambda held: held, (gate_new, down_new))
-    gate_new = jnp.swapaxes(gate_new.reshape(gate_rows.shape), 2, 3)
-    return gate_new, down_new.reshape(w_down.shape)
 
 
 def move_by_scatter(gate_up, w_down, source_slot):
@@ -169,40 +109,10 @@
     return gate_moved.reshape(gate_up.shape), down_moved.reshape(w_down.shape)
 
 
-def shards(
-    tokens,
-    norm_gain,
-    w_qkv,
-    w_out,
-    moe_gain,
-    w_router,
-    gate_up,
-    w_down,
-    lengths,
-    blocks_seen,
-    expert_ids,
-    old_place,
-    new_place,
-):
+def prepare(tokens, norm_gain, w_qkv, lengths, blocks_seen):
     block_rows = tokens.shape[0]
-    model_width = tokens.shape[1]
-    exp_count = lax.axis_size("exp")
     seq_count = lax.axis_size("seq")
     block_index = lax.axis_index("seq")
-    slot_index = lax.axis_index("exp")
-    expert_range = jnp.arange(w_router.shape[1], dtype=jnp.int32)
-
-    slot_old = owner_table(old_place)
-    source_slot = jnp.sum(
-        jnp.where(new_place[:, None] == expert_range[None, :], slot_old[None, :], 0),
-        axis=1,
-        dtype=jnp.int32,
-    )
-    movable = exp_count == 4 and w_down.shape[1] % 9 == 0
-    move = move_by_exchange if movable else move_by_scatter
-    new_gate_up, new_down = move(gate_up, w_down, source_slot)
-
-    ids_all = lax.all_gather(expert_ids, ("seq", "exp"), axis=0, tiled=True)
     heads_here = w_qkv.shape[2] // HEAD_DIM
     query_rows = block_index * block_rows + jnp.arange(block_rows, dtype=jnp.int32)
     query_docs, query_places = doc_layout(lengths, query_rows)
@@ -220,7 +130,6 @@
     pair = jnp.concatenate(
         [key_block.reshape(block_rows, -1), value_block.reshape(block_rows, -1)], axis=1
     )
-    pair_all = gather_xor(pair).reshape(seq_count * block_rows, 2, heads_here, HEAD_DIM)
     order = block_index ^ jnp.arange(seq_count, dtype=jnp.int32)
     key_rows = (
         order[:, None] * block_rows + jnp.arange(block_rows, dtype=jnp.int32)[None, :]
@@ -233,6 +142,32 @@
         & (key_rows[None, :] <= query_rows[:, None])
         & key_seen[None, :]
     )
+    return queries, pair, allowed
+
+
+def layer(
+    queries,
+    pair,
+    allowed,
+    tokens,
+    w_out,
+    moe_gain,
+    w_router,
+    gate_up,
+    w_down,
+    expert_ids,
+    old_place,
+    moving=(),
+):
+    block_rows = tokens.shape[0]
+    model_width = tokens.shape[1]
+    exp_count = lax.axis_size("exp")
+    moving = list(moving)
+    seq_count = lax.axis_size("seq")
+    slot_index = lax.axis_index("exp")
+    expert_range = jnp.arange(w_router.shape[1], dtype=jnp.int32)
+    heads_here = queries.shape[1]
+    pair_all = gather_xor(pair).reshape(seq_count * block_rows, 2, heads_here, HEAD_DIM)
     attended = attend(queries, pair_all[:, 0], pair_all[:, 1], allowed)
     attended = jnp.transpose(attended, (1, 0, 2)).reshape(block_rows, heads_here * HEAD_DIM)
     shard_rows = block_rows // exp_count
@@ -244,11 +179,15 @@
     residual = lax.dynamic_slice_in_dim(tokens, slot_index * shard_rows, shard_rows, 0)
     hidden = (residual.astype(jnp.float32) + head_total).astype(jnp.bfloat16)
     moe_in = rms_scale(hidden, moe_gain).astype(jnp.bfloat16)
-    spread = jnp.broadcast_to(moe_in[None], (exp_count,) + moe_in.shape)
-    block_in = lax.all_to_all(spread, "exp", 0, 0, tiled=True)
-    flat_rows = gather_xor(block_in.reshape(block_rows, model_width)).reshape(-1, model_width)
-
-    ids = jnp.take(ids_all.reshape(seq_count, block_rows, 2), order, axis=0).reshape(-1, 2)
+    named = jnp.pad(expert_ids.astype(jnp.bfloat16), ((0, 0), (0, 126)))
+    labelled = jnp.concatenate([moe_in, named], axis=1)
+    spread = jnp.broadcast_to(labelled[None], (exp_count,) + labelled.shape)
+    block_in = lax.all_to_all(spread, "exp", 0, 0, tiled=True).reshape(block_rows, -1)
+    if moving:
+        block_in, moving[0] = lax.optimization_barrier((block_in, moving[0]))
+    all_rows = gather_xor(block_in).reshape(seq_count * block_rows, -1)
+    flat_rows = all_rows[:, :model_width]
+    ids = all_rows[:, model_width : model_width + 2].astype(jnp.int32)
     logits = jnp.dot(flat_rows, w_router, preferred_element_type=jnp.float32)
     chosen = jnp.sum(
         jnp.where(ids[:, :, None] == expert_range[None, None, :], logits[:, None, :], 0.0),
@@ -265,6 +204,8 @@
     activated = (jax.nn.silu(projected_gate) * projected_up).astype(jnp.bfloat16)
     flat_out = jnp.dot(activated, w_down[0], preferred_element_type=jnp.float32)
     weighted = (flat_out * gating[:, None]).astype(jnp.bfloat16)
+    if moving:
+        weighted, moving[1] = lax.optimization_barrier((weighted, moving[1]))
     summed = reduce_xor(weighted.reshape(seq_count, block_rows, model_width))
     returned = lax.all_to_all(
         summed.astype(jnp.bfloat16).reshape(exp_count, shard_rows, model_width),
@@ -275,7 +216,56 @@
     )
     moe_sum = jnp.sum(returned.astype(jnp.float32), axis=0)
     layer_out = (hidden.astype(jnp.float32) + moe_sum).astype(jnp.bfloat16)
-    return (layer_out, new_gate_up, new_down)
+    return layer_out, moving
+
+
+def shards(
+    tokens,
+    norm_gain,
+    w_qkv,
+    w_out,
+    moe_gain,
+    w_router,
+    gate_up,
+    w_down,
+    lengths,
+    blocks_seen,
+    expert_ids,
+    old_place,
+    new_place,
+):
+    slots = lax.axis_size("exp")
+    slot_old = owner_table(old_place)
+    source_slot = jnp.sum(
+        jnp.where(new_place[:, None] == jnp.arange(slots)[None, :], slot_old[None, :], 0),
+        axis=1,
+        dtype=jnp.int32,
+    )
+    ready = prepare(tokens, norm_gain, w_qkv, lengths, blocks_seen)
+    operands = ready + (
+        tokens, w_out, moe_gain, w_router, gate_up, w_down, expert_ids, old_place,
+    )
+    if slots > 4:
+        moved = move_by_scatter(gate_up, w_down, source_slot)
+        return (layer(*operands)[0],) + moved
+    orders = list(itertools.permutations(range(slots)))
+    weight = slots ** np.arange(slots)
+    codes = jnp.array([int(np.dot(weight, order)) for order in orders], jnp.int32)
+    code = jnp.sum(source_slot * jnp.array(weight, jnp.int32))
+    index = jnp.sum(jnp.where(codes == code, jnp.arange(len(orders)), 0))
+
+    def branch(order):
+        pairs = [(source, slot) for slot, source in enumerate(order)]
+
+        def run(*held):
+            rows = [held[7][0, 0].T, held[7][0, 1].T, held[8][0]]
+            moving = [lax.ppermute(part, "exp", pairs) for part in rows]
+            layer_out, moved = layer(*held, moving=moving)
+            return layer_out, jnp.stack([moved[0].T, moved[1].T])[None], moved[2][None]
+
+        return run
+
+    return lax.switch(index, [branch(order) for order in orders], *operands)
 
 
 def solution(mesh):

time: 553 us -> 438 us (0.79)
  starting transfers between devices: 172 us -> 29.8 us
  waiting for transfers between devices: 88.1 us -> 172 us
  other arithmetic: 101 us -> 20.1 us
  loops' own time: 0.01 us -> 54.7 us
  local copies, waits for them, and re-layouts: 67 us -> 36.8 us
  blocking collectives: 74.7 us -> 88.4 us
  matrix products: 34.9 us -> 26.3 us
    ppermute x44 -> x3, starting transfers between devices: 145 us -> 9.68 us  [run(): moving = [lax.ppermute(part, 'exp', pairs) for part in rows]]
    all_to_all x0 -> x1, blocking collectives: none -> 88.4 us  [layer(): lax.all_to_all(spread, 'exp', 0, 0, tiled=True).reshape(block_rows, -1)]
    all_gather x1 -> x0, blocking collectives: 74.7 us -> none  [shards(): ids_all = lax.all_gather(expert_ids, ('seq', 'exp'), axis=0, tiled=True)]
    unnamed x0 -> x1, loops' own time: none -> 54.7 us
    select_n x24 -> x2, other arithmetic: 47.9 us -> 0.71 us  [the longest x1 0.71 us: layer(): jnp.where(ids[:, 0] == here, gate_first, jnp.where(ids[:, 1] == here, gat...]
    ppermute x12, waiting for transfers between devices: 29.3 us -> 68.7 us  [from_xor(): return lax.ppermute(value, 'seq', [(i, i ^ distance) for i in range(count)])]
    all_to_all x3 -> x2, waiting for transfers between devices: 12.5 us -> 51.1 us  [the longest x1 45 us: layer(): lax.all_to_all(summed.astype(jnp.bfloat16).reshape(exp_count, shard_rows,...]
    dynamic_update_slice x22 -> x0, other arithmetic: 35.2 us -> none  [the longest x11 18.1 us: move_by_exchange(): down_new = lax.dynamic_update_index_in_dim(down_new, fresh[1], at, 0)]
  transfers between devices with their start and end apart: 59 -> 17, of which waited for: 16 -> 13; matrix products, arithmetic and copies ran while one was open for 30% -> 8% of each run, Pallas kernels for 0% -> 0%
where the time goes in v2:
time: 438 us; the launch traced here: 430 us
  waiting for transfers between devices  172 us (39%)
  blocking collectives  88.4 us (20%)
  loops' own time  54.7 us (12%)
  local copies, waits for them, and re-layouts  36.8 us (8%)
  starting transfers between devices  29.8 us (7%)
  matrix products  26.3 us (6%)
  other arithmetic  20.1 us (5%)
    all_to_all x1, blocking collectives, layer(): lax.all_to_all(spread, 'exp', 0, 0, tiled=True).reshape(block_rows, -1)  88.4 us
    ppermute x12, waiting for transfers between devices, from_xor(): return lax.ppermute(value, 'seq', [(i, i ^ distance) for i in range(count)])  68.7 us
    unnamed x1, loops' own time  54.7 us
    ppermute x3, waiting for transfers between devices, run(): moving = [lax.ppermute(part, 'exp', pairs) for part in rows]  52 us
    all_to_all x1, waiting for transfers between devices, layer(): lax.all_to_all(summed.astype(jnp.bfloat16).reshape(exp_count, shard_rows,...  45 us
    dot_general x4, local copies, waits for them, and re-layouts, prepare(): jnp.dot(normed, w_qkv[:, part], preferred_element_type=jnp.float32)  16.2 us
    ppermute x12, starting transfers between devices, from_xor(): return lax.ppermute(value, 'seq', [(i, i ^ distance) for i in range(count)])  11.8 us
    ppermute x3, starting transfers between devices, run(): moving = [lax.ppermute(part, 'exp', pairs) for part in rows]  9.68 us
  transfers between devices with their start and end apart: 17, of which 13 were waited for; matrix products, arithmetic and copies ran while one was open for 8% of the time, Pallas kernels for 0%

profile of v2, /device:TPU:0, one launch (start us, length us, event | category | flops | bytes accessed | tf_op | source)
XLA Modules:
  0.0 429.7 jit_solution(9335538278345554208)
XLA Ops:
  2.4 6.2 %slice_bitcast_fusion.288 = (bf16[512,2304]{0,1:T(8,128)(2,1)}, bf16[512,2304]{0,1:T(8,128)(2,1)}, bf16[512,2304]{0,1:T(8,128)(2,1)}) fusion(bf16[2304,3,512]{2,0,1:T(8,128)(2,1)} %param.41), kind=kLoop, calls=%fused_computation.1777 | loop fusion | bytes 14155776 | tf_op jit(solution)/shard_map/dot_general | solution.py:121
  8.7 2.9 copy.607
  12.7 2.8 copy.605
  17.1 4.3 copy.606
  21.5 2.8 convolution_convert_fusion.24
  29.6 395.9 %conditional.4 = (bf16[1,2,2304,720]{2,3,1,0:T(8,128)(2,1)}, bf16[1,720,2304]{2,1,0:T(8,128)(2,1)}, bf16[32,2304]{1,0:T(8,128)(2,1)S(1)}) conditional(s32[]{:T(128)} %clamp.3, (bf16[128,2304]{1,0:T(8,128)(2,1)S(1)}, pred[128,1024]{0,1:T(8,128)(4,1)}, bf16[128,1024]{0,1:T(8,128)(2,1)S(1)}, ...), branch_computations={%region_9.0_spmd, %region_17.25_spmd, %region_25.33_spmd, %region_... | conditional | flops 10820858880 | bytes 301104032
  62.9 3.0 collective-permute-start.210
  67.5 5.6 %collective-permute-done.210 = bf16[128,1024]{0,1:T(8,128)(2,1)S(1)} collective-permute-done((bf16[128,1024]{0,1:T(8,128)(2,1)S(1)}, bf16[128,1024]{0,1:T(8,128)(2,1)S(1)}, u32[]{:S(2)}, u32[]{:S(2)}) %collective-permute-start.210) | collective-permute-done | bytes 262176 | tf_op jit(solution)/shard_map/cond/branch_14_fun/ppermute | solution.py:74
  73.1 6.3 %collective-permute-done.211 = bf16[128,1024]{0,1:T(8,128)(2,1)S(1)} collective-permute-done((bf16[128,1024]{0,1:T(8,128)(2,1)S(1)}, bf16[128,1024]{0,1:T(8,128)(2,1)S(1)}, u32[]{:S(2)}, u32[]{:S(2)}) %collective-permute-start.211) | collective-permute-done | bytes 262176 | tf_op jit(solution)/shard_map/cond/branch_14_fun/ppermute | solution.py:74
  79.6 2.6 collective-permute-done.213
  82.4 3.5 copy.555
  85.9 4.4 %reshape.1018 = bf16[1024,2,8,64]{0,3,2,1:T(8,128)(2,1)} reshape(bf16[4,2,128,1024]{2,1,0,3:T(2,128)(2,1)} %copy.555) | data formatting | bytes 4194304 | tf_op jit(solution)/shard_map/cond/branch_14_fun/reshape;cond/branch_14_fun/reshape | solution.py:170
  96.5 4.9 %all-to-all-start.42 = ((bf16[4,32,2304]{2,1,0:T(8,128)(2,1)}), bf16[4,32,2304]{2,1,0:T(8,128)(2,1)S(1)}, u32[]{:S(2)}, u32[]{:S(2)}) async-start(bf16[4,32,2304]{2,1,0:T(8,128)(2,1)} %bitcast.2908), calls=%async_computation.42 | async-start | bytes 1179648 | tf_op jit(solution)/shard_map/cond/branch_14_fun/all_to_all | solution.py:175
  101.4 6.2 %slice_bitcast_fusion.168 = (bf16[720,2304]{1,0:T(8,128)(2,1)}, bf16[720,2304]{1,0:T(8,128)(2,1)}) fusion(bf16[1,2,2304,720]{2,3,1,0:T(8,128)(2,1)} %get-tuple-element.755), kind=kLoop, calls=%fused_computation.1055 | loop fusion | bytes 13271040 | tf_op jit(solution)/shard_map/cond/branch_14_fun/transpose | solution.py:261
  107.6 4.8 %collective-permute-start.214 = (bf16[720,2304]{1,0:T(8,128)(2,1)}, bf16[720,2304]{1,0:T(8,128)(2,1)}, u32[]{:S(2)}, u32[]{:S(2)}) collective-permute-start(bf16[720,2304]{1,0:T(8,128)(2,1)} %get-tuple-element.2209), channel_id=1, source_target_pairs={{2,0},{1,1},{0,2},{3,3},{6,4},{5,5},{4,6},{7,7},{10,8},{9,9},{8,10... | collective-permute-start | bytes 9953288 | tf_op jit(solution)/shard_map/cond/branch_14_fun/ppermute | solution.py:262
  112.5 6.1 %all-to-all-done.42 = bf16[4,32,2304]{2,1,0:T(8,128)(2,1)S(1)} async-done(((bf16[4,32,2304]{2,1,0:T(8,128)(2,1)}), bf16[4,32,2304]{2,1,0:T(8,128)(2,1)S(1)}, u32[]{:S(2)}, u32[]{:S(2)}) %all-to-all-start.42) | async-done | bytes 589856 | tf_op jit(solution)/shard_map/cond/branch_14_fun/all_to_all | solution.py:175
  119.0 88.4 %all_to_all.302 = bf16[4,32,2432]{2,1,0:T(8,128)(2,1)S(1)} all-to-all(bf16[4,32,2432]{2,1,0:T(8,128)(2,1)S(1)} %broadcast_in_dim.1165), channel_id=1, replica_groups=mesh['seq'=8,'exp'=4] {'exp'}, dimensions={0} | all-to-all | bytes 1245184 | tf_op jit(solution)/shard_map/cond/branch_14_fun/all_to_all | solution.py:185
  210.9 13.5 %collective-permute-done.215 = bf16[128,2432]{1,0:T(8,128)(2,1)S(1)} collective-permute-done((bf16[128,2432]{1,0:T(8,128)(2,1)S(1)}, bf16[128,2432]{1,0:T(8,128)(2,1)S(1)}, u32[]{:S(2)}, u32[]{:S(2)}) %collective-permute-start.215) | collective-permute-done | bytes 622624 | tf_op jit(solution)/shard_map/cond/branch_14_fun/ppermute | solution.py:74
  224.4 10.4 %collective-permute-done.216 = bf16[128,2432]{1,0:T(8,128)(2,1)S(1)} collective-permute-done((bf16[128,2432]{1,0:T(8,128)(2,1)S(1)}, bf16[128,2432]{1,0:T(8,128)(2,1)S(1)}, u32[]{:S(2)}, u32[]{:S(2)}) %collective-permute-start.216) | collective-permute-done | bytes 622624 | tf_op jit(solution)/shard_map/cond/branch_14_fun/ppermute | solution.py:74
  237.0 2.5 collective-permute-start.219
  245.7 6.6 %fusion.647 = f32[1024,720]{0,1:T(8,128)S(1)} fusion(bf16[1024,2432]{1,0:T(8,128)(2,1)} %bitcast.2687, bf16[1,2,2304,720]{2,3,1,0:T(8,128)(2,1)} %get-tuple-element.755), kind=kOutput, calls=%fused_computation.1047 | convolution fusion | flops 3397386240 | bytes 10985472 | tf_op jit(solution)/shard_map/cond/branch_14_fun/dot_general | solution.py:203
  252.4 3.6 fusion.649
  256.0 6.3 %multiply_convert_fusion.42 = bf16[1024,2304]{1,0:T(8,128)(2,1)S(1)} fusion(f32[1024]{0:T(1024)S(1)} %bitcast.3126, f32[1024,720]{0,1:T(8,128)S(1)} %fusion.647, f32[1024,720]{0,1:T(8,128)S(1)} %fusion.649, bf16[1,720,2304]{2,1,0:T(8,128)(2,1)} %get-tuple-element.758), kind=kOutput, calls=%fused_computation.1038 | convolution fusion | flops 3406528512 | bytes 13938688 | tf_op jit(solution)/shard_map/cond/branch_14_fun/dot_general | solution.py:205
  262.3 52.0 %collective-permute-done.219 = bf16[720,2304]{1,0:T(8,128)(2,1)} collective-permute-done((bf16[720,2304]{1,0:T(8,128)(2,1)}, bf16[720,2304]{1,0:T(8,128)(2,1)}, u32[]{:S(2)}, u32[]{:S(2)}) %collective-permute-start.219) | collective-permute-done | bytes 3317792 | tf_op jit(solution)/shard_map/cond/branch_14_fun/ppermute | solution.py:262
  314.5 2.3 collective-permute-start.220
  316.8 2.2 collective-permute-done.221
  323.3 12.7 %collective-permute-done.222 = bf16[128,2304]{1,0:T(8,128)(2,1)S(1)} collective-permute-done((bf16[128,2304]{1,0:T(8,128)(2,1)S(1)}, bf16[128,2304]{1,0:T(8,128)(2,1)S(1)}, u32[]{:S(2)}, u32[]{:S(2)}) %collective-permute-start.222) | collective-permute-done | bytes 589856 | tf_op jit(solution)/shard_map/cond/branch_14_fun/ppermute | solution.py:74
  336.0 12.3 %collective-permute-done.223 = bf16[128,2304]{1,0:T(8,128)(2,1)S(1)} collective-permute-done((bf16[128,2304]{1,0:T(8,128)(2,1)S(1)}, bf16[128,2304]{1,0:T(8,128)(2,1)S(1)}, u32[]{:S(2)}, u32[]{:S(2)}) %collective-permute-start.223) | collective-permute-done | bytes 589856 | tf_op jit(solution)/shard_map/cond/branch_14_fun/ppermute | solution.py:74
  349.5 3.5 all-to-all-start.44
  353.0 6.4 %maximum_bitcast_fusion.14 = bf16[1,2,2304,720]{2,3,1,0:T(8,128)(2,1)} fusion(bf16[1,2304,720]{1,2,0:T(8,128)(2,1)} %bitcast.619, bf16[1,2304,720]{1,2,0:T(8,128)(2,1)} %bitcast.605), kind=kLoop, calls=%fused_computation.1039 | loop fusion | flops 3317760 | bytes 13271040 | tf_op jit(solution)/shard_map/cond/branch_14_fun/broadcast_in_dim | solution.py:264
  359.3 45.0 %all-to-all-done.44 = bf16[4,32,2304]{2,1,0:T(8,128)(2,1)S(1)} async-done(((bf16[4,32,2304]{2,1,0:T(8,128)(2,1)}), bf16[4,32,2304]{2,1,0:T(8,128)(2,1)S(1)}, u32[]{:S(2)}, u32[]{:S(2)}) %all-to-all-start.44) | async-done | bytes 589856 | tf_op jit(solution)/shard_map/cond/branch_14_fun/all_to_all | solution.py:210
  425.6 3.9 copy.777
  (115 shorter events, 35.3 us)
Async XLA Ops:
  0.6 23.7 %copy-start = (s32[1,8]{1,0:T(1,128)S(1)}, s32[1,8]{1,0:T(1,128)}, u32[]{:S(2)}) copy-start(s32[1,8]{1,0:T(1,128)} %param.48) | copy-start | bytes 100
  8.7 2.9 copy-start.3
  21.4 5.4 %copy-start.107 = (s32[4]{0:T(128)S(1)}, s32[4]{0:T(128)}, u32[]{:S(2)}) copy-start(s32[4]{0:T(128)} %param.50) | copy-start | bytes 52
  21.4 5.5 %copy-start.106 = (s32[4]{0:T(128)S(1)}, s32[4]{0:T(128)}, u32[]{:S(2)}) copy-start(s32[4]{0:T(128)} %param.51) | copy-start | bytes 52
  21.4 5.6 %copy-start.109 = (s32[4]{0:T(128)S(1)}, s32[4]{0:T(128)}, u32[]{:S(2)}) copy-start(s32[4]{0:T(128)} %constant.725.clone) | copy-start | bytes 52
  21.4 6.3 %copy-start.108 = (s32[24]{0:T(128)S(1)}, s32[24]{0:T(128)}, u32[]{:S(2)}) copy-start(s32[24]{0:T(128)} %constant.724.clone) | copy-start | bytes 292
  21.4 7.5 %copy-start.2 = (bf16[512,2304]{1,0:T(8,128)(2,1)S(1)}, bf16[512,2304]{1,0:T(8,128)(2,1)}, u32[]{:S(2)}) copy-start(bf16[512,2304]{1,0:T(8,128)(2,1)} %param.42) | copy-start | bytes 7077892
  21.4 7.5 %copy-start.76 = (bf16[2304]{0:T(1024)(128)(2,1)S(1)}, bf16[2304]{0:T(1024)(128)(2,1)}, u32[]{:S(2)}) copy-start(bf16[2304]{0:T(1024)(128)(2,1)} %param.43) | copy-start | bytes 13828
  21.4 7.5 %copy-start.77 = (s32[32,2]{0,1:T(2,128)S(1)}, s32[32,2]{0,1:T(2,128)}, u32[]{:S(2)}) copy-start(s32[32,2]{0,1:T(2,128)} %param.49) | copy-start | bytes 772
  21.4 7.5 %copy-start.105 = (bf16[2304,4]{0,1:T(4,128)(2,1)S(1)}, bf16[2304,4]{0,1:T(4,128)(2,1)}, u32[]{:S(2)}) copy-start(bf16[2304,4]{0,1:T(4,128)(2,1)} %param.44) | copy-start | bytes 55300
  62.9 10.1 %collective-permute-start.210 = (bf16[128,1024]{0,1:T(8,128)(2,1)S(1)}, bf16[128,1024]{0,1:T(8,128)(2,1)S(1)}, u32[]{:S(2)}, u32[]{:S(2)}) collective-permute-start(bf16[128,1024]{0,1:T(8,128)(2,1)S(1)} %get-tuple-element.750), channel_id=1, source_target_pairs={{0,8},{4,12},{8,0},{12,4},{16,24},{20,28},{24,16},{28,20},{1,9},{5... | collective-permute-start | bytes 786440 | tf_op jit(solution)/shard_map/cond/branch_14_fun/ppermute | solution.py:74
  65.9 13.4 %collective-permute-start.211 = (bf16[128,1024]{0,1:T(8,128)(2,1)S(1)}, bf16[128,1024]{0,1:T(8,128)(2,1)S(1)}, u32[]{:S(2)}, u32[]{:S(2)}) collective-permute-start(bf16[128,1024]{0,1:T(8,128)(2,1)S(1)} %get-tuple-element.750), channel_id=1, source_target_pairs={{0,16},{4,20},{8,24},{12,28},{16,0},{20,4},{24,8},{28,12},{1,17},{... | collective-permute-start | bytes 786440 | tf_op jit(solution)/shard_map/cond/branch_14_fun/ppermute | solution.py:74
  67.5 11.9 %collective-permute-start.212 = (bf16[128,1024]{0,1:T(8,128)(2,1)S(1)}, bf16[128,1024]{0,1:T(8,128)(2,1)S(1)}, u32[]{:S(2)}, u32[]{:S(2)}) collective-permute-start(bf16[128,1024]{0,1:T(8,128)(2,1)S(1)} %get-tuple-element.750), channel_id=1, source_target_pairs={{0,24},{4,28},{8,16},{12,20},{16,8},{20,12},{24,0},{28,4},{1,25},{... | collective-permute-start | bytes 786440 | tf_op jit(solution)/shard_map/cond/branch_14_fun/ppermute | solution.py:74
  79.5 2.7 collective-permute-start.213
  96.5 22.1 %all-to-all-start.42 = ((bf16[4,32,2304]{2,1,0:T(8,128)(2,1)}), bf16[4,32,2304]{2,1,0:T(8,128)(2,1)S(1)}, u32[]{:S(2)}, u32[]{:S(2)}) async-start(bf16[4,32,2304]{2,1,0:T(8,128)(2,1)} %bitcast.2908), calls=%async_computation.42 | async-start | bytes 1179648 | tf_op jit(solution)/shard_map/cond/branch_14_fun/all_to_all | solution.py:175
  107.6 99.8 %collective-permute-start.214 = (bf16[720,2304]{1,0:T(8,128)(2,1)}, bf16[720,2304]{1,0:T(8,128)(2,1)}, u32[]{:S(2)}, u32[]{:S(2)}) collective-permute-start(bf16[720,2304]{1,0:T(8,128)(2,1)} %get-tuple-element.2209), channel_id=1, source_target_pairs={{2,0},{1,1},{0,2},{3,3},{6,4},{5,5},{4,6},{7,7},{10,8},{9,9},{8,10... | collective-permute-start | bytes 9953288 | tf_op jit(solution)/shard_map/cond/branch_14_fun/ppermute | solution.py:262
  207.4 17.0 %collective-permute-start.215 = (bf16[128,2432]{1,0:T(8,128)(2,1)S(1)}, bf16[128,2432]{1,0:T(8,128)(2,1)S(1)}, u32[]{:S(2)}, u32[]{:S(2)}) collective-permute-start(bf16[128,2432]{1,0:T(8,128)(2,1)S(1)} %bitcast.2829), channel_id=1, source_target_pairs={{0,8},{4,12},{8,0},{12,4},{16,24},{20,28},{24,16},{28,20},{1,9},{5... | collective-permute-start | bytes 1867784 | tf_op jit(solution)/shard_map/cond/branch_14_fun/ppermute | solution.py:74
  208.6 26.2 %collective-permute-start.216 = (bf16[128,2432]{1,0:T(8,128)(2,1)S(1)}, bf16[128,2432]{1,0:T(8,128)(2,1)S(1)}, u32[]{:S(2)}, u32[]{:S(2)}) collective-permute-start(bf16[128,2432]{1,0:T(8,128)(2,1)S(1)} %bitcast.2830), channel_id=1, source_target_pairs={{0,16},{4,20},{8,24},{12,28},{16,0},{20,4},{24,8},{28,12},{1,17},{... | collective-permute-start | bytes 1867784 | tf_op jit(solution)/shard_map/cond/branch_14_fun/ppermute | solution.py:74
  209.4 27.0 %collective-permute-start.217 = (bf16[128,2432]{1,0:T(8,128)(2,1)S(1)}, bf16[128,2432]{1,0:T(8,128)(2,1)S(1)}, u32[]{:S(2)}, u32[]{:S(2)}) collective-permute-start(bf16[128,2432]{1,0:T(8,128)(2,1)S(1)} %bitcast.2831), channel_id=1, source_target_pairs={{0,24},{4,28},{8,16},{12,20},{16,8},{20,12},{24,0},{28,4},{1,25},{... | collective-permute-start | bytes 1867784 | tf_op jit(solution)/shard_map/cond/branch_14_fun/ppermute | solution.py:74
  236.9 4.8 %collective-permute-start.218 = (bf16[4,128,2432]{2,1,0:T(8,128)(2,1)S(1)}, bf16[4,128,2432]{2,1,0:T(8,128)(2,1)S(1)}, u32[]{:S(2)}, u32[]{:S(2)}) collective-permute-start(bf16[4,128,2432]{2,1,0:T(8,128)(2,1)S(1)} %get-tuple-element.2211), channel_id=1, source_target_pairs={{0,4},{4,0},{8,12},{12,8},{16,20},{20,16},{24,28},{28,24},{1,5},{5... | collective-permute-start | bytes 7471112 | tf_op jit(solution)/shard_map/cond/branch_14_fun/ppermute | solution.py:74
  237.0 77.3 %collective-permute-start.219 = (bf16[720,2304]{1,0:T(8,128)(2,1)}, bf16[720,2304]{1,0:T(8,128)(2,1)}, u32[]{:S(2)}, u32[]{:S(2)}) collective-permute-start(bf16[720,2304]{1,0:T(8,128)(2,1)} %get-tuple-element.2208), channel_id=1, source_target_pairs={{2,0},{1,1},{0,2},{3,3},{6,4},{5,5},{4,6},{7,7},{10,8},{9,9},{8,10... | collective-permute-start | bytes 9953288 | tf_op jit(solution)/shard_map/cond/branch_14_fun/ppermute | solution.py:262
  242.2 10.1 %slice-start.28 = ((s8[6635520]{0:T(1024)(128)(4,1)}), s8[2441216]{0:T(1024)(128)(4,1)S(1)}, s32[]{:S(2)}) async-start(s8[6635520]{0:T(1024)(128)(4,1)} %bitcast.2583), calls=%async_computation.100 | async-start | bytes 4882432
  245.6 6.7 %slice-start.29 = ((s8[6635520]{0:T(1024)(128)(4,1)}), s8[4194304]{0:T(1024)(128)(4,1)S(1)}, s32[]{:S(2)}) async-start(s8[6635520]{0:T(1024)(128)(4,1)} %bitcast.2583), calls=%async_computation.101 | async-start | bytes 8388608
  245.7 6.7 %copy-start.33 = (bf16[4,2,128,2432]{3,2,1,0:T(8,128)(2,1)S(1)}, bf16[4,2,128,2432]{3,2,1,0:T(8,128)(2,1)}, u32[]{:S(2)}) copy-start(bf16[4,2,128,2432]{3,2,1,0:T(8,128)(2,1)} %copy-done.32) | copy-start | bytes 14942212
  314.4 4.6 %collective-permute-start.221 = (bf16[4,128,2304]{2,1,0:T(8,128)(2,1)S(1)}, bf16[4,128,2304]{2,1,0:T(8,128)(2,1)S(1)}, u32[]{:S(2)}, u32[]{:S(2)}) collective-permute-start(bf16[4,128,2304]{2,1,0:T(8,128)(2,1)S(1)} %slice_bitcast_fusion.170), channel_id=1, source_target_pairs={{0,4},{4,0},{8,12},{12,8},{16,20},{20,16},{24,28},{28,24},{1,5},{5... | collective-permute-start | bytes 7077896 | tf_op jit(solution)/shard_map/cond/branch_14_fun/ppermute | solution.py:74
  314.5 90.0 %collective-permute-start.220 = (bf16[720,2304]{1,0:T(8,128)(2,1)}, bf16[720,2304]{1,0:T(8,128)(2,1)}, u32[]{:S(2)}, u32[]{:S(2)}) collective-permute-start(bf16[720,2304]{1,0:T(8,128)(2,1)} %bitcast.615), channel_id=1, source_target_pairs={{2,0},{1,1},{0,2},{3,3},{6,4},{5,5},{4,6},{7,7},{10,8},{9,9},{8,10... | collective-permute-start | bytes 9953288 | tf_op jit(solution)/shard_map/cond/branch_14_fun/ppermute | solution.py:262
  319.8 16.2 %collective-permute-start.222 = (bf16[128,2304]{1,0:T(8,128)(2,1)S(1)}, bf16[128,2304]{1,0:T(8,128)(2,1)S(1)}, u32[]{:S(2)}, u32[]{:S(2)}) collective-permute-start(bf16[128,2304]{1,0:T(8,128)(2,1)S(1)} %get-tuple-element.2212), channel_id=1, source_target_pairs={{0,8},{4,12},{8,0},{12,4},{16,24},{20,28},{24,16},{28,20},{1,9},{5... | collective-permute-start | bytes 1769480 | tf_op jit(solution)/shard_map/cond/branch_14_fun/ppermute | solution.py:74
  320.6 27.7 %collective-permute-start.223 = (bf16[128,2304]{1,0:T(8,128)(2,1)S(1)}, bf16[128,2304]{1,0:T(8,128)(2,1)S(1)}, u32[]{:S(2)}, u32[]{:S(2)}) collective-permute-start(bf16[128,2304]{1,0:T(8,128)(2,1)S(1)} %get-tuple-element.2214), channel_id=1, source_target_pairs={{0,16},{4,20},{8,24},{12,28},{16,0},{20,4},{24,8},{28,12},{1,17},{... | collective-permute-start | bytes 1769480 | tf_op jit(solution)/shard_map/cond/branch_14_fun/ppermute | solution.py:74
  322.2 26.2 %collective-permute-start.224 = (bf16[128,2304]{1,0:T(8,128)(2,1)S(1)}, bf16[128,2304]{1,0:T(8,128)(2,1)S(1)}, u32[]{:S(2)}, u32[]{:S(2)}) collective-permute-start(bf16[128,2304]{1,0:T(8,128)(2,1)S(1)} %get-tuple-element.2213), channel_id=1, source_target_pairs={{0,24},{4,28},{8,16},{12,20},{16,8},{20,12},{24,0},{28,4},{1,25},{... | collective-permute-start | bytes 1769480 | tf_op jit(solution)/shard_map/cond/branch_14_fun/ppermute | solution.py:74
  349.5 54.9 %all-to-all-start.44 = ((bf16[4,32,2304]{2,1,0:T(8,128)(2,1)}), bf16[4,32,2304]{2,1,0:T(8,128)(2,1)S(1)}, u32[]{:S(2)}, u32[]{:S(2)}) async-start(bf16[4,32,2304]{2,1,0:T(8,128)(2,1)} %bitcast.629), calls=%async_computation.44 | async-start | bytes 1179648 | tf_op jit(solution)/shard_map/cond/branch_14_fun/all_to_all | solution.py:210
  425.6 4.0 copy-start.79
  425.6 3.9 copy-start.1
  (5 other events, 12.6 us)
